TPU v7x, 256 devices: a whole 4x4x8 slice. The times are simulated.
256 devices in a mesh: section: 4 (over z_hi, core), tp: 64 (over x, y, z_lo).
Axes of the slice: x: 4, y: 4, z: 8 (z_hi: 2, z_lo: 4; z = z_hi * 4 + z_lo), core: 2. Of those that a mesh axis runs over, the one named last changes fastest.
Arguments:
- travelling_inputs: bfloat16 [4, 512, 3072], P('section', 'tp'), may hold values from -6 to 6
- travelling_region: int32 [4, 512], P('section', 'tp'), may hold values 0 or 1
- arriving_tiles: bfloat16 [4, 512, 3072], P('section', 'tp'), may hold values from -6 to 6
- arriving_region: int32 [4, 512], P('section', 'tp'), may hold values 0 or 1
- prompt_embeddings: bfloat16 [2048, 3584], P(('section', 'tp')), may hold values from -6 to 6
- prompt_tally: int32 [1], replicated, may hold values from 512 to 2048
- adaptive_norm_weights: bfloat16 [4, 9216, 3584], P('section', 'tp'), may hold values from -0.09375 to 0.09375
- expansion_weights: bfloat16 [4, 12288, 3072], P('section', 'tp'), may hold values from -0.109375 to 0.109375
- contraction_weights: bfloat16 [4, 12288, 3072], P('section', 'tp'), may hold values from -0.0546875 to 0.0546875
Outputs:
- finished: bfloat16 [4, 512, 3072], P('section', 'tp')
- state: bfloat16 [4, 512, 3072], P('section', 'tp')
All inputs are finite; a program needn't handle non-finite values. No bound on the sum of `travelling_region` or of `arriving_region` on one device may be relied on, other than what follows from the above.
Results may differ from a plain program's by a relative error of at most 0.01.
Values may be sent and summed in bfloat16 or wider, within the bound.
No kernel may reach another device: no remote copies, remote signals or barrier semaphores. Data moves between devices by JAX's collectives and lax.ppermute only.
A program may use at most 64 MiB of HBM per device.

v0:
```python
import jax
import jax.numpy as jnp
from jax import lax
from jax.sharding import PartitionSpec as P


def partner(block, axis, distance):
    count = lax.axis_size(axis)
    route = []
    for low in range(count):
        high = low | 1 << distance
        if high != low and high < count:
            route += [(low, high), (high, low)]
    return lax.ppermute(block, axis, route)


def from_behind(block, axis, distance):
    devices = range(lax.axis_size(axis))
    route = [(i - distance, i) for i in devices if i - distance in devices]
    return lax.ppermute(block, axis, route)


def per_device(
    travelling_inputs,
    travelling_region,
    arriving_tiles,
    arriving_region,
    prompt_embeddings,
    prompt_tally,
    adaptive_norm_weights,
    expansion_weights,
    contraction_weights,
):
    sections = lax.axis_size("section")
    section_id = lax.axis_index("section")
    tp_total = lax.axis_size("tp")
    tp_levels = tp_total.bit_length() - 1
    low_levels = min(4, tp_levels)
    tp_id = lax.axis_index("tp")
    count_rows = prompt_embeddings.shape[0]
    first_row = lax.axis_index(("section", "tp")) * count_rows
    keep = (first_row + lax.iota(jnp.int32, count_rows) < prompt_tally[0]).astype(jnp.bfloat16)
    partial_value = jnp.dot(keep[None, :], prompt_embeddings, preferred_element_type=jnp.float32)[0]
    pooled = lax.psum(partial_value, ("section", "tp"))
    pooled = pooled / prompt_tally[0].astype(jnp.float32)
    normed = pooled * lax.rsqrt(jnp.mean(pooled * pooled) + 1e-06)
    cond = jax.nn.silu(normed).astype(jnp.bfloat16)
    local_modes = jnp.dot(adaptive_norm_weights[0], cond, preferred_element_type=jnp.float32)
    modes = lax.all_gather(local_modes, "tp", axis=0, tiled=True)
    expansion_breadth = travelling_inputs.shape[2]
    shift = modes[:expansion_breadth]
    scale = modes[expansion_breadth : 2 * expansion_breadth]
    gate = modes[2 * expansion_breadth :]
    up_local = expansion_weights[0]
    down_local = contraction_weights[0]
    for level in range(low_levels, tp_levels):
        other_up, other_down = partner((up_local, down_local), "tp", level)
        up_local = jnp.concatenate([up_local, other_up], axis=0)
        down_local = jnp.concatenate([down_local, other_down], axis=0)

    def bit_set(level):
        return tp_id // (1 << level) % 2 == 1

    def group_sum(totals):
        for level in reversed(range(low_levels)):
            middle = totals.shape[0] // 2
            lower = totals[:middle]
            upper = totals[middle:]
            upper_side = bit_set(level)
            kept = jnp.where(upper_side, upper, lower)
            sent = jnp.where(upper_side, lower, upper)
            totals = kept + partner(sent, "tp", level)
        return totals

    entering, entering_mask = (
        lax.all_gather(arriving_tiles, "section", axis=0, tiled=True),
        lax.all_gather(arriving_region.astype(jnp.bfloat16), "section", axis=0, tiled=True),
    )
    waiting_tiles = travelling_inputs[0]
    held_patch_mask = travelling_region[0].astype(jnp.bfloat16)
    is_first = section_id == 0
    outputs = []
    for tick in range(sections):
        values = waiting_tiles.astype(jnp.float32)
        center = jnp.mean(values, axis=1, keepdims=True)
        spread = jnp.mean((values - center) ** 2, axis=1, keepdims=True)
        normed_rows = (values - center) * lax.rsqrt(spread + 1e-06)
        inputs = (normed_rows * (1.0 + scale) + shift).astype(jnp.bfloat16)
        buffer = inputs
        for group_level in range(low_levels):
            others = partner(buffer, "tp", group_level)
            buffer = jnp.where(
                bit_set(group_level),
                jnp.concatenate([others, buffer], axis=0),
                jnp.concatenate([buffer, others], axis=0),
            )
        raised = lax.dot_general(
            buffer, up_local, (((1,), (1,)), ((), ())), preferred_element_type=jnp.float32
        )
        hidden = jax.nn.gelu(raised, approximate=True).astype(jnp.bfloat16)
        result = group_sum(jnp.dot(hidden, down_local, preferred_element_type=jnp.float32))
        produced = (values + held_patch_mask.astype(jnp.float32)[:, None] * gate * result).astype(
            jnp.bfloat16
        )
        outputs.append(produced)
        moved, moved_mask = from_behind((produced, held_patch_mask), "section", 1)
        waiting_tiles = jnp.where(is_first, entering[tick], moved)
        held_patch_mask = jnp.where(is_first, entering_mask[tick], moved_mask)
    stacked = jnp.stack(outputs)
    received = lax.all_to_all(stacked, "section", split_axis=0, concat_axis=0, tiled=True)
    finished = received[sections - 1][None]
    return (finished, waiting_tiles[None])


def solution(mesh):
    placed = (
        P("section", "tp", None),
        P("section", "tp"),
        P("section", "tp", None),
        P("section", "tp"),
        P(("section", "tp"), None),
        P(),
        P("section", "tp", None),
        P("section", "tp", None),
        P("section", "tp", None),
    )
    return jax.shard_map(
        per_device,
        mesh=mesh,
        in_specs=placed,
        out_specs=(P("section", "tp", None), P("section", "tp", None)),
        check_vma=False,
    )
```

profile of v0, /device:TPU:1, one launch (start us, length us, event | category | flops | bytes accessed | tf_op | source)
XLA Modules:
  0.0 870.9 jit_solution(16643747929930484877)
XLA Ops:
  4.5 122.0 %psum.7 = f32[3584]{0:T(1024)S(1)} all-reduce(f32[3584]{0:T(1024)S(1)} %convolution_reduce_fusion), channel_id=1, replica_groups=mesh['section'=4,'tp'=64] {'section','tp'}, use_global_device_ids=true, to_apply=%region_0.0 | all-reduce | flops 3584 | bytes 28672 | tf_op jit(solution)/shard_map/psum | solution.py:44
  130.3 309.2 %all-reduce = f32[9216]{0:T(1024)S(1)} all-reduce(f32[9216]{0:T(1024)S(1)} %dynamic-update-slice), channel_id=1, replica_groups=mesh['section'=4,'tp'=64] {'tp'}, use_global_device_ids=true, to_apply=%add | all-reduce | flops 9216 | bytes 73728
  443.6 3.1 pad_maximum_fusion.3
  446.7 2.9 collective-permute-start.7
  453.9 5.4 collective-permute-done.1
  461.1 4.8 collective-permute-done.2
  468.0 8.5 collective-permute-done.3
  476.5 21.6 %collective-permute-done.7 = bf16[384,3072]{1,0:T(8,128)(2,1)} collective-permute-done((bf16[384,3072]{1,0:T(8,128)(2,1)}, bf16[384,3072]{1,0:T(8,128)(2,1)}, u32[]{:S(2)}, u32[]{:S(2)}) %collective-permute-start.7) | collective-permute-done | bytes 2359328 | tf_op jit(solution)/shard_map/ppermute | solution.py:14
  498.1 7.3 fusion.38
  505.6 12.7 %collective-permute-done.8 = f32[64,3072]{1,0:T(8,128)S(1)} collective-permute-done((f32[64,3072]{1,0:T(8,128)S(1)}, f32[64,3072]{1,0:T(8,128)S(1)}, u32[]{:S(2)}, u32[]{:S(2)}) %collective-permute-start.8) | collective-permute-done | bytes 786464 | tf_op jit(solution)/shard_map/ppermute | solution.py:14
  518.7 9.1 %collective-permute-done.9 = f32[32,3072]{1,0:T(8,128)S(1)} collective-permute-done((f32[32,3072]{1,0:T(8,128)S(1)}, f32[32,3072]{1,0:T(8,128)S(1)}, u32[]{:S(2)}, u32[]{:S(2)}) %collective-permute-start.9) | collective-permute-done | bytes 393248 | tf_op jit(solution)/shard_map/ppermute | solution.py:14
  528.0 5.8 collective-permute-done.10
  534.2 3.8 collective-permute-done.11
  538.1 63.6 %collective-permute-start.12 = (bf16[8,3072]{1,0:T(8,128)(2,1)S(1)}, bf16[8,3072]{1,0:T(8,128)(2,1)S(1)}, u32[]{:S(2)}, u32[]{:S(2)}) collective-permute-start(bf16[8,3072]{1,0:T(8,128)(2,1)S(1)} %fusion.108), channel_id=1, source_target_pairs={{0,64},{64,128},{128,192},{1,65},{65,129},{129,193},{2,66},{66,130... | collective-permute-start | bytes 147464 | tf_op jit(solution)/shard_map/ppermute | solution.py:20
  601.7 8.4 all_gather.10
  610.7 2.9 collective-permute-done.14
  613.7 6.7 collective-permute-done.15
  620.6 5.2 collective-permute-done.16
  626.0 10.1 %collective-permute-done.17 = bf16[64,3072]{1,0:T(8,128)(2,1)} collective-permute-done((bf16[64,3072]{1,0:T(8,128)(2,1)S(1)}, bf16[64,3072]{1,0:T(8,128)(2,1)}, u32[]{:S(2)}, u32[]{:S(2)}) %collective-permute-start.17) | collective-permute-done | bytes 393248 | tf_op jit(solution)/shard_map/ppermute | solution.py:14
  636.0 7.1 fusion.47
  643.6 17.2 %collective-permute-done.18 = f32[64,3072]{1,0:T(8,128)S(1)} collective-permute-done((f32[64,3072]{1,0:T(8,128)S(1)}, f32[64,3072]{1,0:T(8,128)S(1)}, u32[]{:S(2)}, u32[]{:S(2)}) %collective-permute-start.18) | collective-permute-done | bytes 786464 | tf_op jit(solution)/shard_map/ppermute | solution.py:14
  662.0 5.7 collective-permute-done.19
  668.0 8.0 collective-permute-start.13
  676.0 7.8 all-gather
  683.9 4.0 collective-permute-done.21
  688.1 4.1 collective-permute-start.22
  693.9 2.9 collective-permute-done.24
  696.8 2.7 collective-permute-start.25
  699.5 4.7 collective-permute-done.25
  705.9 4.7 collective-permute-done.26
  712.4 9.5 %collective-permute-done.27 = bf16[64,3072]{1,0:T(8,128)(2,1)} collective-permute-done((bf16[64,3072]{1,0:T(8,128)(2,1)S(1)}, bf16[64,3072]{1,0:T(8,128)(2,1)}, u32[]{:S(2)}, u32[]{:S(2)}) %collective-permute-start.27) | collective-permute-done | bytes 393248 | tf_op jit(solution)/shard_map/ppermute | solution.py:14
  721.9 7.1 fusion.56
  730.7 16.9 %collective-permute-done.28 = f32[64,3072]{1,0:T(8,128)S(1)} collective-permute-done((f32[64,3072]{1,0:T(8,128)S(1)}, f32[64,3072]{1,0:T(8,128)S(1)}, u32[]{:S(2)}, u32[]{:S(2)}) %collective-permute-start.28) | collective-permute-done | bytes 786464 | tf_op jit(solution)/shard_map/ppermute | solution.py:14
  749.2 6.2 collective-permute-done.29
  756.3 8.4 collective-permute-start.23
  765.4 3.3 collective-permute-done.31
  768.7 6.2 collective-permute-start.32
  776.7 3.5 collective-permute-done.34
  781.3 6.4 collective-permute-done.35
  787.9 6.0 collective-permute-done.36
  795.8 9.1 %collective-permute-done.37 = bf16[64,3072]{1,0:T(8,128)(2,1)} collective-permute-done((bf16[64,3072]{1,0:T(8,128)(2,1)S(1)}, bf16[64,3072]{1,0:T(8,128)(2,1)}, u32[]{:S(2)}, u32[]{:S(2)}) %collective-permute-start.37) | collective-permute-done | bytes 393248 | tf_op jit(solution)/shard_map/ppermute | solution.py:14
  804.9 7.1 fusion.65
  814.1 16.4 %collective-permute-done.38 = f32[64,3072]{1,0:T(8,128)S(1)} collective-permute-done((f32[64,3072]{1,0:T(8,128)S(1)}, f32[64,3072]{1,0:T(8,128)S(1)}, u32[]{:S(2)}, u32[]{:S(2)}) %collective-permute-start.38) | collective-permute-done | bytes 786464 | tf_op jit(solution)/shard_map/ppermute | solution.py:14
  830.8 7.4 collective-permute-done.39
  838.4 8.1 collective-permute-start.33
  851.3 7.8 collective-permute-start.42
  859.7 3.4 all-to-all-start
  863.7 6.6 all-to-all-done
  (153 shorter events, 46.1 us)
Async XLA Ops:
  0.6 129.1 %copy-start = (bf16[1,144,3584]{2,1,0:T(8,128)(2,1)S(1)}, bf16[1,144,3584]{2,1,0:T(8,128)(2,1)}, u32[]{:S(2)}) copy-start(bf16[1,144,3584]{2,1,0:T(8,128)(2,1)} %param.15) | copy-start | bytes 3096580
  0.6 440.9 %collective-permute-start.4 = (bf16[192,3072]{1,0:T(8,128)(2,1)}, bf16[192,3072]{1,0:T(8,128)(2,1)}, u32[]{:S(2)}, u32[]{:S(2)}) collective-permute-start(bf16[192,3072]{1,0:T(8,128)(2,1)} %bitcast.88), channel_id=1, source_target_pairs={{0,16},{16,0},{1,17},{17,1},{2,18},{18,2},{3,19},{19,3},{4,20},{20... | collective-permute-start | bytes 3538952 | tf_op jit(solution)/shard_map/ppermute | solution.py:14
  2.8 440.8 %collective-permute-start.6 = (bf16[192,3072]{1,0:T(8,128)(2,1)}, bf16[192,3072]{1,0:T(8,128)(2,1)}, u32[]{:S(2)}, u32[]{:S(2)}) collective-permute-start(bf16[192,3072]{1,0:T(8,128)(2,1)} %bitcast.82), channel_id=1, source_target_pairs={{0,16},{16,0},{1,17},{17,1},{2,18},{18,2},{3,19},{19,3},{4,20},{20... | collective-permute-start | bytes 3538952 | tf_op jit(solution)/shard_map/ppermute | solution.py:14
  443.5 33.0 %collective-permute-start.5 = (bf16[384,3072]{1,0:T(8,128)(2,1)S(1)}, bf16[384,3072]{1,0:T(8,128)(2,1)}, u32[]{:S(2)}, u32[]{:S(2)}) collective-permute-start(bf16[384,3072]{1,0:T(8,128)(2,1)S(1)} %pad_maximum_fusion.2), channel_id=1, source_target_pairs={{0,32},{32,0},{1,33},{33,1},{2,34},{34,2},{3,35},{35,3},{4,36},{36... | collective-permute-start | bytes 7077896 | tf_op jit(solution)/shard_map/ppermute | solution.py:14
  446.7 51.4 %collective-permute-start.7 = (bf16[384,3072]{1,0:T(8,128)(2,1)}, bf16[384,3072]{1,0:T(8,128)(2,1)}, u32[]{:S(2)}, u32[]{:S(2)}) collective-permute-start(bf16[384,3072]{1,0:T(8,128)(2,1)} %pad_maximum_fusion.3), channel_id=1, source_target_pairs={{0,32},{32,0},{1,33},{33,1},{2,34},{34,2},{3,35},{35,3},{4,36},{36... | collective-permute-start | bytes 7077896 | tf_op jit(solution)/shard_map/ppermute | solution.py:14
  449.7 3.1 collective-permute-start
  453.8 5.6 collective-permute-start.1
  461.1 4.8 collective-permute-start.2
  468.0 8.5 collective-permute-start.3
  505.5 12.8 %collective-permute-start.8 = (f32[64,3072]{1,0:T(8,128)S(1)}, f32[64,3072]{1,0:T(8,128)S(1)}, u32[]{:S(2)}, u32[]{:S(2)}) collective-permute-start(f32[64,3072]{1,0:T(8,128)S(1)} %slice_select_fusion.3), channel_id=1, source_target_pairs={{0,8},{8,0},{1,9},{9,1},{2,10},{10,2},{3,11},{11,3},{4,12},{12,4},... | collective-permute-start | bytes 2359304 | tf_op jit(solution)/shard_map/ppermute | solution.py:14
  518.5 83.2 %copy-start.8 = (bf16[1,8,3072]{2,1,0:T(8,128)(2,1)S(1)}, bf16[1,8,3072]{2,1,0:T(8,128)(2,1)}, u32[]{:S(2)}) copy-start(bf16[1,8,3072]{2,1,0:T(8,128)(2,1)} %param.11) | copy-start | bytes 147460
  518.5 91.9 %copy-start.4 = (f32[3072]{0:T(1024)S(1)}, f32[3072]{0:T(1024)}, u32[]{:S(2)}) copy-start(f32[3072]{0:T(1024)} %copy-done.3) | copy-start | bytes 36868
  518.5 91.9 %copy-start.6 = (f32[3072]{0:T(1024)S(1)}, f32[3072]{0:T(1024)}, u32[]{:S(2)}) copy-start(f32[3072]{0:T(1024)} %copy-done.5) | copy-start | bytes 36868
  518.6 9.2 %collective-permute-start.9 = (f32[32,3072]{1,0:T(8,128)S(1)}, f32[32,3072]{1,0:T(8,128)S(1)}, u32[]{:S(2)}, u32[]{:S(2)}) collective-permute-start(f32[32,3072]{1,0:T(8,128)S(1)} %slice_select_fusion.7), channel_id=1, source_target_pairs={{0,4},{4,0},{1,5},{5,1},{2,6},{6,2},{3,7},{7,3},{8,12},{12,8},{9,1... | collective-permute-start | bytes 1179656 | tf_op jit(solution)/shard_map/ppermute | solution.py:14
  527.9 5.9 collective-permute-start.10
  533.9 4.1 collective-permute-start.11
  538.1 72.0 %collective-permute-start.12 = (bf16[8,3072]{1,0:T(8,128)(2,1)S(1)}, bf16[8,3072]{1,0:T(8,128)(2,1)S(1)}, u32[]{:S(2)}, u32[]{:S(2)}) collective-permute-start(bf16[8,3072]{1,0:T(8,128)(2,1)S(1)} %fusion.108), channel_id=1, source_target_pairs={{0,64},{64,128},{128,192},{1,65},{65,129},{129,193},{2,66},{66,130... | collective-permute-start | bytes 147464 | tf_op jit(solution)/shard_map/ppermute | solution.py:20
  610.6 3.0 collective-permute-start.14
  613.6 6.8 collective-permute-start.15
  620.5 5.3 collective-permute-start.16
  625.8 10.2 %collective-permute-start.17 = (bf16[64,3072]{1,0:T(8,128)(2,1)S(1)}, bf16[64,3072]{1,0:T(8,128)(2,1)}, u32[]{:S(2)}, u32[]{:S(2)}) collective-permute-start(bf16[64,3072]{1,0:T(8,128)(2,1)S(1)} %maximum_select_fusion.33), channel_id=1, source_target_pairs={{0,8},{8,0},{1,9},{9,1},{2,10},{10,2},{3,11},{11,3},{4,12},{12,4},... | collective-permute-start | bytes 1179656 | tf_op jit(solution)/shard_map/ppermute | solution.py:14
  643.2 17.6 %collective-permute-start.18 = (f32[64,3072]{1,0:T(8,128)S(1)}, f32[64,3072]{1,0:T(8,128)S(1)}, u32[]{:S(2)}, u32[]{:S(2)}) collective-permute-start(f32[64,3072]{1,0:T(8,128)S(1)} %slice_select_fusion.2), channel_id=1, source_target_pairs={{0,8},{8,0},{1,9},{9,1},{2,10},{10,2},{3,11},{11,3},{4,12},{12,4},... | collective-permute-start | bytes 2359304 | tf_op jit(solution)/shard_map/ppermute | solution.py:14
  661.0 6.7 collective-permute-start.19
  667.8 15.9 %collective-permute-start.20 = (f32[16,3072]{1,0:T(8,128)S(1)}, f32[16,3072]{1,0:T(8,128)S(1)}, u32[]{:S(2)}, u32[]{:S(2)}) collective-permute-start(f32[16,3072]{1,0:T(8,128)S(1)} %slice_select_fusion.10), channel_id=1, source_target_pairs={{0,2},{2,0},{1,3},{3,1},{4,6},{6,4},{5,7},{7,5},{8,10},{10,8},{9,1... | collective-permute-start | bytes 589832 | tf_op jit(solution)/shard_map/ppermute | solution.py:14
  668.0 16.0 %collective-permute-start.13 = (bf16[8]{0:T(256)(128)(2,1)S(1)}, bf16[8]{0:T(256)(128)(2,1)S(1)}, u32[]{:S(2)}, u32[]{:S(2)}) collective-permute-start(bf16[8]{0:T(256)(128)(2,1)S(1)} %get-tuple-element.15), channel_id=1, source_target_pairs={{0,64},{64,128},{128,192},{1,65},{65,129},{129,193},{2,66},{66,130... | collective-permute-start | bytes 56 | tf_op jit(solution)/shard_map/ppermute | solution.py:20
  683.8 4.2 collective-permute-start.21
  688.1 5.2 collective-permute-start.22
  693.8 3.0 collective-permute-start.24
  696.8 7.4 collective-permute-start.25
  704.3 6.2 collective-permute-start.26
  710.6 11.3 %collective-permute-start.27 = (bf16[64,3072]{1,0:T(8,128)(2,1)S(1)}, bf16[64,3072]{1,0:T(8,128)(2,1)}, u32[]{:S(2)}, u32[]{:S(2)}) collective-permute-start(bf16[64,3072]{1,0:T(8,128)(2,1)S(1)} %maximum_select_fusion.34), channel_id=1, source_target_pairs={{0,8},{8,0},{1,9},{9,1},{2,10},{10,2},{3,11},{11,3},{4,12},{12,4},... | collective-permute-start | bytes 1179656 | tf_op jit(solution)/shard_map/ppermute | solution.py:14
  729.1 18.5 %collective-permute-start.28 = (f32[64,3072]{1,0:T(8,128)S(1)}, f32[64,3072]{1,0:T(8,128)S(1)}, u32[]{:S(2)}, u32[]{:S(2)}) collective-permute-start(f32[64,3072]{1,0:T(8,128)S(1)} %slice_select_fusion.1), channel_id=1, source_target_pairs={{0,8},{8,0},{1,9},{9,1},{2,10},{10,2},{3,11},{11,3},{4,12},{12,4},... | collective-permute-start | bytes 2359304 | tf_op jit(solution)/shard_map/ppermute | solution.py:14
  747.8 7.7 collective-permute-start.29
  755.5 9.1 %collective-permute-start.30 = (f32[16,3072]{1,0:T(8,128)S(1)}, f32[16,3072]{1,0:T(8,128)S(1)}, u32[]{:S(2)}, u32[]{:S(2)}) collective-permute-start(f32[16,3072]{1,0:T(8,128)S(1)} %slice_select_fusion.9), channel_id=1, source_target_pairs={{0,2},{2,0},{1,3},{3,1},{4,6},{6,4},{5,7},{7,5},{8,10},{10,8},{9,1... | collective-permute-start | bytes 589832 | tf_op jit(solution)/shard_map/ppermute | solution.py:14
  756.3 9.1 %collective-permute-start.23 = (bf16[8]{0:T(256)(128)(2,1)S(1)}, bf16[8]{0:T(256)(128)(2,1)S(1)}, u32[]{:S(2)}, u32[]{:S(2)}) collective-permute-start(bf16[8]{0:T(256)(128)(2,1)S(1)} %get-tuple-element.9), channel_id=1, source_target_pairs={{0,64},{64,128},{128,192},{1,65},{65,129},{129,193},{2,66},{66,130... | collective-permute-start | bytes 56 | tf_op jit(solution)/shard_map/ppermute | solution.py:20
  764.7 3.9 collective-permute-start.31
  768.7 7.4 collective-permute-start.32
  776.6 3.6 collective-permute-start.34
  780.2 7.5 collective-permute-start.35
  787.8 6.1 collective-permute-start.36
  794.0 11.0 %collective-permute-start.37 = (bf16[64,3072]{1,0:T(8,128)(2,1)S(1)}, bf16[64,3072]{1,0:T(8,128)(2,1)}, u32[]{:S(2)}, u32[]{:S(2)}) collective-permute-start(bf16[64,3072]{1,0:T(8,128)(2,1)S(1)} %maximum_select_fusion.35), channel_id=1, source_target_pairs={{0,8},{8,0},{1,9},{9,1},{2,10},{10,2},{3,11},{11,3},{4,12},{12,4},... | collective-permute-start | bytes 1179656 | tf_op jit(solution)/shard_map/ppermute | solution.py:14
  812.1 18.4 %collective-permute-start.38 = (f32[64,3072]{1,0:T(8,128)S(1)}, f32[64,3072]{1,0:T(8,128)S(1)}, u32[]{:S(2)}, u32[]{:S(2)}) collective-permute-start(f32[64,3072]{1,0:T(8,128)S(1)} %slice_select_fusion), channel_id=1, source_target_pairs={{0,8},{8,0},{1,9},{9,1},{2,10},{10,2},{3,11},{11,3},{4,12},{12,4},... | collective-permute-start | bytes 2359304 | tf_op jit(solution)/shard_map/ppermute | solution.py:14
  830.7 7.5 collective-permute-start.39
  838.3 8.2 collective-permute-start.40
  838.4 10.4 %collective-permute-start.33 = (bf16[8]{0:T(256)(128)(2,1)S(1)}, bf16[8]{0:T(256)(128)(2,1)S(1)}, u32[]{:S(2)}, u32[]{:S(2)}) collective-permute-start(bf16[8]{0:T(256)(128)(2,1)S(1)} %get-tuple-element.5), channel_id=1, source_target_pairs={{0,64},{64,128},{128,192},{1,65},{65,129},{129,193},{2,66},{66,130... | collective-permute-start | bytes 56 | tf_op jit(solution)/shard_map/ppermute | solution.py:20
  846.5 4.6 collective-permute-start.41
  851.3 11.8 %collective-permute-start.42 = (bf16[8,3072]{1,0:T(8,128)(2,1)S(1)}, bf16[8,3072]{1,0:T(8,128)(2,1)S(1)}, u32[]{:S(2)}, u32[]{:S(2)}) collective-permute-start(bf16[8,3072]{1,0:T(8,128)(2,1)S(1)} %fusion.111), channel_id=1, source_target_pairs={{0,64},{64,128},{128,192},{1,65},{65,129},{129,193},{2,66},{66,130... | collective-permute-start | bytes 147464 | tf_op jit(solution)/shard_map/ppermute | solution.py:20
  859.7 10.6 %all-to-all-start = ((bf16[4,8,3072]{2,1,0:T(8,128)(2,1)}), bf16[4,8,3072]{2,1,0:T(8,128)(2,1)S(1)}, u32[]{:S(2)}, u32[]{:S(2)}) async-start(bf16[4,8,3072]{2,1,0:T(8,128)(2,1)} %pad_maximum_fusion.4), calls=%async_computation | async-start | bytes 393216 | tf_op jit(solution)/shard_map/all_to_all | solution.py:110
  (7 other events, 47.7 us)
where the time goes:
time: 872 us; the launch traced here: 871 us
  blocking collectives  447 us (51%)
  waiting for transfers between devices  235 us (27%)
  starting transfers between devices  135 us (15%)
  matrix products  29.8 us (3%)
  other arithmetic  17.4 us (2%)
    unnamed x1, blocking collectives  309 us
    ppermute x36, waiting for transfers between devices, partner(): return lax.ppermute(block, axis, route)  226 us
    psum x1, blocking collectives, per_device(): pooled = lax.psum(partial_value, ('section', 'tp'))  122 us
    ppermute x7, starting transfers between devices, from_behind(): return lax.ppermute(block, axis, route)  106 us
    dot_general x4, matrix products, per_device(): jnp.dot(hidden, down_local, preferred_element_type=jnp.float32)  28.5 us
    ppermute x36, starting transfers between devices, partner(): return lax.ppermute(block, axis, route)  25.6 us
  transfers between devices with their start and end apart: 44, of which 34 were waited for; matrix products, arithmetic and copies ran while one was open for 2% of the time, Pallas kernels for 0%

commit v1 on v0

v1 whole, which is shorter than its diff:
```python
import functools

import jax
import jax.numpy as jnp
import numpy as np
from jax import lax
from jax.experimental import pallas as pl
from jax.experimental.pallas import tpu as pltpu
from jax.sharding import Mesh, PartitionSpec as P

f32 = jnp.float32
bf16 = jnp.bfloat16

SIZES = {"zh": 2, "core": 2, "xh": 2, "xl": 2, "yh": 2, "yl": 2, "z": 4}
SECTION = ("zh", "core")
TP = ("xh", "xl", "yh", "yl", "z")
PLANE = ("xh", "xl", "yh", "yl")
GROUP = ("xh", "z")
GROUP_SIZE = 8
SECTIONS = 4
LANES = 128


def from_neighbour(block, axis, distance):
    route = [((i + distance) % 4, i) for i in range(4)]
    return lax.ppermute(block, (axis + "h", axis + "l"), route)


def between_sections(block, edges):
    return lax.ppermute(block, SECTION, edges)


def exchange(block, axes):
    count = int(np.prod([SIZES[a] for a in axes]))
    copies = jnp.broadcast_to(block[None], (count,) + block.shape)
    return lax.all_to_all(copies, axes, 0, 0)


def ffn_kernel(pieces, half, x_ref, mod_ref, *refs):
    weights = refs[:pieces]
    out_ref, up, down, inputs, hidden, sem = refs[pieces:]
    lifts, drops = [], []
    for i, w in enumerate(weights):
        rows = pl.ds(i * half, half)
        lifts.append(pltpu.make_async_copy(w.at[pl.ds(0, half)], up.at[rows], sem.at[0, i]))
        drops.append(pltpu.make_async_copy(w.at[pl.ds(half, half)], down.at[rows], sem.at[1, i]))
    for copy in lifts:
        copy.start()
    for copy in drops:
        copy.start()
    values = x_ref[...].astype(f32)
    center = jnp.mean(values, axis=1, keepdims=True)
    moved = values - center
    spread = jnp.mean(moved * moved, axis=1, keepdims=True)
    inputs[...] = (
        moved * lax.rsqrt(spread + 1e-06) * (1.0 + mod_ref[1:2]) + mod_ref[0:1]
    ).astype(bf16)
    total = pieces * half
    step = 256
    arrived = 0
    for at in range(0, total, step):
        while arrived * half < at + step:
            lifts[arrived].wait()
            arrived += 1
        raised = lax.dot_general(
            inputs[...],
            up[at : at + step],
            (((1,), (1,)), ((), ())),
            preferred_element_type=f32,
        )
        hidden[:, at : at + step] = jax.nn.gelu(raised, approximate=True).astype(bf16)
    for copy in drops:
        copy.wait()
    for at in range(0, out_ref.shape[1], step):
        out_ref[:, at : at + step] = jnp.dot(
            hidden[...], down[:, at : at + step], preferred_element_type=f32
        ).astype(bf16)


def ffn(tokens, mod, weights):
    rows, breadth = tokens.shape
    pieces = len(weights)
    half = weights[0].shape[0] // 2
    total = pieces * half
    whole = pl.BlockSpec(memory_space=pltpu.VMEM)
    return pl.pallas_call(
        functools.partial(ffn_kernel, pieces, half),
        out_shape=jax.ShapeDtypeStruct((rows, breadth), bf16),
        in_specs=[whole, whole] + [pl.BlockSpec(memory_space=pl.ANY)] * pieces,
        out_specs=whole,
        scratch_shapes=[
            pltpu.VMEM((total, breadth), bf16),
            pltpu.VMEM((total, breadth), bf16),
            pltpu.VMEM((rows, breadth), bf16),
            pltpu.VMEM((rows, total), bf16),
            pltpu.SemaphoreType.DMA((2, pieces)),
        ],
        compiler_params=pltpu.CompilerParams(vmem_limit_bytes=40 * 1024 * 1024),
        cost_estimate=pl.CostEstimate(
            flops=4 * rows * total * breadth,
            bytes_accessed=4 * total * breadth + 4 * rows * breadth,
            transcendentals=rows * total,
        ),
    )(tokens, mod, *weights)


def spread_weights(up, down):
    middle = up.shape[0] // 2
    first = jnp.concatenate([up[:middle], down[:middle]], axis=0)
    second = jnp.concatenate([up[middle:], down[middle:]], axis=0)
    xa = from_neighbour(first, "x", 1)
    xb = from_neighbour(second, "x", -1)
    yp_first = from_neighbour(first, "y", 1)
    ym_second = from_neighbour(second, "y", -1)
    yp_second = from_neighbour(second, "y", 1)
    ym_first = from_neighbour(first, "y", -1)
    xa_yp = from_neighbour(yp_first, "x", 1)
    xb_ym = from_neighbour(ym_second, "x", -1)
    y2_first = from_neighbour(yp_first, "y", 1)
    y2_second = from_neighbour(ym_second, "y", -1)
    xa_ym = from_neighbour(ym_first, "x", 1)
    xb_yp = from_neighbour(yp_second, "x", -1)
    xa_y2 = from_neighbour(y2_first, "x", 1)
    xb_y2 = from_neighbour(y2_second, "x", -1)
    return [
        first, second, xa, xb, yp_first, ym_second, yp_second, ym_first,
        xa_yp, xb_ym, y2_first, y2_second, xa_ym, xb_yp, xa_y2, xb_y2,
    ]


def condition(prompt_embeddings, prompt_tally, adaptive_norm_weights):
    count_rows, encoded = prompt_embeddings.shape
    first_row = lax.axis_index(SECTION + TP) * count_rows
    keep = (first_row + lax.iota(jnp.int32, count_rows) < prompt_tally[0]).astype(bf16)
    partial = jnp.dot(keep[None, :], prompt_embeddings, preferred_element_type=f32)
    partial = partial.reshape(encoded // LANES, LANES)
    partial = jnp.sum(exchange(partial, PLANE), axis=0)
    pooled = jnp.sum(exchange(partial, ("zh", "core", "z")), axis=0)
    pooled = pooled / prompt_tally[0].astype(f32)
    normed = pooled * lax.rsqrt(jnp.mean(pooled * pooled) + 1e-06)
    cond = jax.nn.silu(normed).astype(bf16).reshape(encoded)
    local = jnp.dot(adaptive_norm_weights, cond, preferred_element_type=f32)
    columns = local.shape[0]
    rows = -(-columns // LANES)
    local = jnp.pad(local, (0, rows * LANES - columns)).reshape(rows, LANES)
    modes = exchange(local, TP)
    return modes.reshape(modes.shape[0], rows * LANES)[:, :columns].reshape(3, -1)


def per_device(
    travelling_inputs,
    travelling_region,
    arriving_tiles,
    arriving_region,
    prompt_embeddings,
    prompt_tally,
    adaptive_norm_weights,
    expansion_weights,
    contraction_weights,
):
    section_id = lax.axis_index(SECTION)
    is_first = section_id == 0
    tokens, breadth = travelling_inputs.shape[1:]

    def with_mask(values, region):
        column = jnp.broadcast_to(region.astype(bf16)[:, None], (tokens, LANES))
        return jnp.concatenate([values, column], axis=1)

    arriving = with_mask(arriving_tiles[0], arriving_region[0])
    waiting = with_mask(travelling_inputs[0], travelling_region[0])
    entering = [arriving] + [between_sections(arriving, [(s, 0)]) for s in range(1, SECTIONS)]
    mod = condition(prompt_embeddings, prompt_tally, adaptive_norm_weights[0])
    weights = spread_weights(expansion_weights[0], contraction_weights[0])
    finished = None
    for tick in range(SECTIONS):
        gathered = exchange(waiting[:, :breadth], GROUP)
        partial = ffn(gathered.reshape(GROUP_SIZE * tokens, breadth), mod, weights)
        parts = lax.all_to_all(partial.reshape(GROUP_SIZE, tokens, breadth), GROUP, 0, 0)
        result = jnp.sum(parts.astype(f32), axis=0)
        mask = waiting[:, breadth:]
        produced = (
            waiting[:, :breadth].astype(f32) + mask[:, :1].astype(f32) * mod[2][None] * result
        ).astype(bf16)
        produced = jnp.concatenate([produced, mask], axis=1)
        edges = [(s, s + 1) for s in range(SECTIONS - 1)]
        if tick == 0:
            moved = between_sections(produced, edges + [(SECTIONS - 1, 0)])
            finished = moved
        else:
            moved = between_sections(produced, edges)
            if tick < SECTIONS - 1:
                left = between_sections(produced[:, :breadth], [(SECTIONS - 1, tick)])
            else:
                left = produced[:, :breadth]
            finished = jnp.where(section_id == tick, left, finished[:, :breadth])
        waiting = jnp.where(is_first, entering[tick], moved)
    return finished[None], waiting[None, :, :breadth]


def solution(mesh):
    fine = Mesh(mesh.devices.reshape(tuple(SIZES.values())), tuple(SIZES))
    placed = (
        P(SECTION, TP, None),
        P(SECTION, TP),
        P(SECTION, TP, None),
        P(SECTION, TP),
        P(SECTION + TP, None),
        P(),
        P(SECTION, TP, None),
        P(SECTION, TP, None),
        P(SECTION, TP, None),
    )
    return jax.shard_map(
        per_device,
        mesh=fine,
        in_specs=placed,
        out_specs=(P(SECTION, TP, None), P(SECTION, TP, None)),
        check_vma=False,
    )
```

time: 872 us -> 408 us (0.47)
  blocking collectives: 447 us -> 145 us
  waiting for transfers between devices: 235 us -> 103 us
  starting transfers between devices: 135 us -> 93.2 us
  Pallas kernels: 0 us -> 37.5 us
  matrix products: 29.8 us -> 0.48 us
    unnamed x1 -> x0, blocking collectives: 309 us -> none
    ppermute x43 -> x23, waiting for transfers between devices: 229 us -> 47 us  [the longest x14 42.7 us: from_neighbour(): return lax.ppermute(block, (axis + 'h', axis + 'l'), route)]
    all_to_all x0 -> x5, blocking collectives: none -> 145 us  [exchange(): return lax.all_to_all(copies, axes, 0, 0)]
    psum x1 -> x0, blocking collectives: 122 us -> none  [per_device(): pooled = lax.psum(partial_value, ('section', 'tp'))]
    ppermute x43 -> x23, starting transfers between devices: 132 us -> 57.9 us  [the longest x9 37.1 us: between_sections(): return lax.ppermute(block, SECTION, edges)]
    all_to_all x1 -> x6, waiting for transfers between devices: 6.56 us -> 56.3 us  [the longest x4 36.1 us: per_device(): lax.all_to_all(partial.reshape(GROUP_SIZE, tokens, breadth), GROUP, 0, 0)]
    pallas_call x0 -> x4, Pallas kernels: none -> 37.5 us  [ffn(): pl.pallas_call(functools.partial(ffn_kernel, pieces, half), out_shape=jax...]
    all_to_all x1 -> x6, starting transfers between devices: 3.35 us -> 35.3 us  [the longest x2 18.1 us: exchange(): return lax.all_to_all(copies, axes, 0, 0)]
  transfers between devices with their start and end apart: 44 -> 29, of which waited for: 34 -> 12; matrix products, arithmetic and copies ran while one was open for 2% -> 4% of each run, Pallas kernels for 0% -> 0%
where the time goes in v1:
time: 408 us; the launch traced here: 407 us
  blocking collectives  145 us (36%)
  waiting for transfers between devices  103 us (25%)
  starting transfers between devices  93.2 us (23%)
  Pallas kernels  37.5 us (9%)
  other arithmetic  14.9 us (4%)
  local copies, waits for them, and re-layouts  10 us (2%)
    all_to_all x5, blocking collectives, exchange(): return lax.all_to_all(copies, axes, 0, 0)  145 us
    ppermute x14, waiting for transfers between devices, from_neighbour(): return lax.ppermute(block, (axis + 'h', axis + 'l'), route)  42.7 us
    pallas_call x4, Pallas kernels, ffn(): pl.pallas_call(functools.partial(ffn_kernel, pieces, half), out_shape=jax...  37.5 us
    ppermute x9, starting transfers between devices, between_sections(): return lax.ppermute(block, SECTION, edges)  37.1 us
    all_to_all x4, waiting for transfers between devices, per_device(): lax.all_to_all(partial.reshape(GROUP_SIZE, tokens, breadth), GROUP, 0, 0)  36.1 us
    ppermute x14, starting transfers between devices, from_neighbour(): return lax.ppermute(block, (axis + 'h', axis + 'l'), route)  20.8 us
    all_to_all x2, waiting for transfers between devices, exchange(): return lax.all_to_all(copies, axes, 0, 0)  20.2 us
    all_to_all x2, starting transfers between devices, exchange(): return lax.all_to_all(copies, axes, 0, 0)  18.1 us
  transfers between devices with their start and end apart: 29, of which 12 were waited for; matrix products, arithmetic and copies ran while one was open for 4% of the time, Pallas kernels for 0%

profile of v1, /device:TPU:1, one launch (start us, length us, event | category | flops | bytes accessed | tf_op | source)
XLA Modules:
  0.0 406.6 jit_solution(12345048213917543055)
XLA Ops:
  0.6 1.8 slice_bitcast_fusion
  2.6 2.2 collective-permute-start.5
  4.9 1.5 collective-permute-start.4
  6.4 1.4 collective-permute-start.6
  7.9 1.2 collective-permute-start.3
  9.7 20.2 %collective-permute-done.5.refs_5_ = bf16[192,3072]{1,0:T(8,128)(2,1)} collective-permute-done((bf16[192,3072]{1,0:T(8,128)(2,1)S(1)}, bf16[192,3072]{1,0:T(8,128)(2,1)}, u32[]{:S(2)}, u32[]{:S(2)}) %collective-permute-start.5) | collective-permute-done | bytes 1179680 | tf_op jit(solution)/shard_map/ppermute | solution.py:26
  30.0 4.3 %collective-permute-start.2 = (bf16[192,3072]{1,0:T(8,128)(2,1)S(1)}, bf16[192,3072]{1,0:T(8,128)(2,1)}, u32[]{:S(2)}, u32[]{:S(2)}) collective-permute-start(bf16[192,3072]{1,0:T(8,128)(2,1)S(1)} %pad_maximum_fusion.refs_0_), channel_id=1, source_target_pairs={{16,0},{32,16},{48,32},{0,48},{17,1},{33,17},{49,33},{1,49},{18,2}... | collective-permute-start | bytes 3538952 | tf_op jit(solution)/shard_map/ppermute | solution.py:26
  34.3 22.4 %collective-permute-done.6.refs_6_ = bf16[192,3072]{1,0:T(8,128)(2,1)} collective-permute-done((bf16[192,3072]{1,0:T(8,128)(2,1)S(1)}, bf16[192,3072]{1,0:T(8,128)(2,1)}, u32[]{:S(2)}, u32[]{:S(2)}) %collective-permute-start.6) | collective-permute-done | bytes 1179680 | tf_op jit(solution)/shard_map/ppermute | solution.py:26
  56.6 1.4 collective-permute-start.9
  58.1 2.8 collective-permute-start.10
  61.0 28.3 %all_to_all.55 = f32[16,28,128]{2,1,0:T(8,128)} all-to-all(f32[16,28,128]{2,1,0:T(8,128)S(1)} %broadcast_in_dim.25), channel_id=1, replica_groups=mesh['zh'=2,'core'=2,'xh'=2,'xl'=2,'yh'=2,'yl'=2,'z'=4] {'xh','xl','yh',..., dimensions={0} | all-to-all | bytes 458752 | tf_op jit(solution)/shard_map/all_to_all | solution.py:36
  91.1 11.8 %all-to-all-start.1 = ((f32[16,28,128]{2,1,0:T(8,128)}), f32[16,28,128]{2,1,0:T(8,128)}, u32[]{:S(2)}, u32[]{:S(2)}) async-start(f32[16,28,128]{2,1,0:T(8,128)} %broadcast_in_dim.26), calls=%async_computation.1 | async-start | bytes 524288 | tf_op jit(solution)/shard_map/all_to_all | solution.py:36
  102.9 9.7 %all-to-all-done.1 = f32[16,28,128]{2,1,0:T(8,128)} async-done(((f32[16,28,128]{2,1,0:T(8,128)}), f32[16,28,128]{2,1,0:T(8,128)}, u32[]{:S(2)}, u32[]{:S(2)}) %all-to-all-start.1) | async-done | bytes 229408 | tf_op jit(solution)/shard_map/all_to_all | solution.py:36
  115.5 1.0 collective-permute-start.13
  116.4 1.7 collective-permute-start.12
  118.2 2.7 collective-permute-start.14
  121.2 73.2 %all_to_all.56 = f32[64,2,128]{2,1,0:T(2,128)} all-to-all(f32[64,2,128]{2,1,0:T(2,128)S(1)} %broadcast_in_dim.28), channel_id=1, replica_groups=mesh['zh'=2,'core'=2,'xh'=2,'xl'=2,'yh'=2,'yl'=2,'z'=4] {'xh','xl','yh',..., dimensions={0} | all-to-all | bytes 131072 | tf_op jit(solution)/shard_map/all_to_all | solution.py:36
  195.2 6.3 %all-to-all-start.3 = ((bf16[8,8,3072]{2,1,0:T(8,128)(2,1)}), bf16[8,8,3072]{2,1,0:T(8,128)(2,1)}, u32[]{:S(2)}, u32[]{:S(2)}) async-start(bf16[8,8,3072]{2,1,0:T(8,128)(2,1)} %broadcast_in_dim.29), calls=%async_computation.3 | async-start | bytes 786432 | tf_op jit(solution)/shard_map/all_to_all | solution.py:36
  202.4 10.5 %all-to-all-done.3 = bf16[8,8,3072]{2,1,0:T(8,128)(2,1)} async-done(((bf16[8,8,3072]{2,1,0:T(8,128)(2,1)}), bf16[8,8,3072]{2,1,0:T(8,128)(2,1)}, u32[]{:S(2)}, u32[]{:S(2)}) %all-to-all-start.3) | async-done | bytes 393248 | tf_op jit(solution)/shard_map/all_to_all | solution.py:36
  213.0 10.1 %shard_map.104 = bf16[64,3072]{1,0:T(8,128)(2,1)S(1)} custom-call(bf16[64,3072]{1,0:T(8,128)(2,1)} %bitcast.14.x_ref, f32[3,3072]{1,0:T(4,128)S(1)} %reshape.84.mod_ref, bf16[192,3072]{1,0:T(8,128)(2,1)S(1)} %pad_maximum_fusion.refs_0_, bf16[192,3072]{1,0:T(8,128)(2,1)S(1)} %pad_maximum_fusion.1.refs_1_, bf16[192,3072]{1,0:T(8,128)(2,1)} %collective-permute-done.2.refs_2_, ...), custom_call_target="tpu_custom_call" | custom-call | flops 1207959552 | bytes 19660800 | tf_op jit(solution)/shard_map/pallas_call | solution.py:86
  223.8 4.8 %all-to-all-start.4 = ((bf16[8,8,3072]{2,1,0:T(8,128)(2,1)}), bf16[8,8,3072]{2,1,0:T(8,128)(2,1)}, u32[]{:S(2)}, u32[]{:S(2)}) async-start(bf16[8,8,3072]{2,1,0:T(8,128)(2,1)} %bitcast.62), calls=%async_computation.4 | async-start | bytes 786432 | tf_op jit(solution)/shard_map/all_to_all | solution.py:178
  229.2 9.8 %all-to-all-done.4 = bf16[8,8,3072]{2,1,0:T(8,128)(2,1)} async-done(((bf16[8,8,3072]{2,1,0:T(8,128)(2,1)}), bf16[8,8,3072]{2,1,0:T(8,128)(2,1)}, u32[]{:S(2)}, u32[]{:S(2)}) %all-to-all-start.4) | async-done | bytes 393248 | tf_op jit(solution)/shard_map/all_to_all | solution.py:178
  239.0 1.1 convert_reduce_fusion.3
  241.5 9.0 %collective-permute-start.16 = (bf16[8,3200]{1,0:T(8,128)(2,1)}, bf16[8,3200]{1,0:T(8,128)(2,1)S(1)}, u32[]{:S(2)}, u32[]{:S(2)}) collective-permute-start(bf16[8,3200]{1,0:T(8,128)(2,1)} %pad_maximum_fusion.3), channel_id=1, source_target_pairs={{0,64},{64,128},{128,192},{192,0},{1,65},{65,129},{129,193},{193,1... | collective-permute-start | bytes 153608 | tf_op jit(solution)/shard_map/ppermute | solution.py:30
  252.7 1.5 broadcast_select_fusion.2
  254.2 13.2 %all_to_all.57 = bf16[8,8,3072]{2,1,0:T(8,128)(2,1)S(1)} all-to-all(bf16[8,8,3072]{2,1,0:T(8,128)(2,1)S(1)} %broadcast_in_dim.31), channel_id=1, replica_groups=mesh['zh'=2,'core'=2,'xh'=2,'xl'=2,'yh'=2,'yl'=2,'z'=4] {'xh','z'}, dimensions={0} | all-to-all | bytes 786432 | tf_op jit(solution)/shard_map/all_to_all | solution.py:36
  267.3 9.1 %shard_map.105 = bf16[64,3072]{1,0:T(8,128)(2,1)S(1)} custom-call(bf16[64,3072]{1,0:T(8,128)(2,1)S(1)} %bitcast.63, f32[3,3072]{1,0:T(4,128)S(1)} %reshape.84.mod_ref, bf16[192,3072]{1,0:T(8,128)(2,1)S(1)} %pad_maximum_fusion.refs_0_, bf16[192,3072]{1,0:T(8,128)(2,1)S(1)} %pad_maximum_fusion.1.refs_1_, bf16[192,3072]{1,0:T(8,128)(2,1)} %collective-permute-done.2.refs_2_, ...), custom_call_target="tpu_custom_call" | custom-call | flops 1207959552 | bytes 19660800 | tf_op jit(solution)/shard_map/pallas_call | solution.py:86
  277.2 4.7 %all-to-all-start.6 = ((bf16[8,8,3072]{2,1,0:T(8,128)(2,1)}), bf16[8,8,3072]{2,1,0:T(8,128)(2,1)}, u32[]{:S(2)}, u32[]{:S(2)}) async-start(bf16[8,8,3072]{2,1,0:T(8,128)(2,1)} %bitcast.60), calls=%async_computation.6 | async-start | bytes 786432 | tf_op jit(solution)/shard_map/all_to_all | solution.py:178
  282.5 6.1 %collective-permute-start.1 = (bf16[8,3200]{1,0:T(8,128)(2,1)}, bf16[8,3200]{1,0:T(8,128)(2,1)}, u32[]{:S(2)}, u32[]{:S(2)}) collective-permute-start(bf16[8,3200]{1,0:T(8,128)(2,1)} %get-tuple-element.9), channel_id=1, source_target_pairs={{64,0},{65,1},{66,2},{67,3},{68,4},{69,5},{70,6},{71,7},{72,8},{73... | collective-permute-start | bytes 153608 | tf_op jit(solution)/shard_map/ppermute | solution.py:30
  289.3 3.0 all-to-all-done.6
  292.3 1.1 convert_reduce_fusion.2
  294.8 8.8 %collective-permute-start.17 = (bf16[8,3200]{1,0:T(8,128)(2,1)S(1)}, bf16[8,3200]{1,0:T(8,128)(2,1)S(1)}, u32[]{:S(2)}, u32[]{:S(2)}) collective-permute-start(bf16[8,3200]{1,0:T(8,128)(2,1)S(1)} %pad_maximum_fusion.4), channel_id=1, source_target_pairs={{0,64},{64,128},{128,192},{1,65},{65,129},{129,193},{2,66},{66,130... | collective-permute-start | bytes 153608 | tf_op jit(solution)/shard_map/ppermute | solution.py:30
  303.7 1.2 collective-permute-done.17
  304.9 15.0 %all_to_all.58 = bf16[8,8,3072]{2,1,0:T(8,128)(2,1)S(1)} all-to-all(bf16[8,8,3072]{2,1,0:T(8,128)(2,1)S(1)} %broadcast_in_dim.32), channel_id=1, replica_groups=mesh['zh'=2,'core'=2,'xh'=2,'xl'=2,'yh'=2,'yl'=2,'z'=4] {'xh','z'}, dimensions={0} | all-to-all | bytes 786432 | tf_op jit(solution)/shard_map/all_to_all | solution.py:36
  319.9 9.1 %shard_map.106 = bf16[64,3072]{1,0:T(8,128)(2,1)S(1)} custom-call(bf16[64,3072]{1,0:T(8,128)(2,1)S(1)} %bitcast.64, f32[3,3072]{1,0:T(4,128)S(1)} %reshape.84.mod_ref, bf16[192,3072]{1,0:T(8,128)(2,1)S(1)} %pad_maximum_fusion.refs_0_, bf16[192,3072]{1,0:T(8,128)(2,1)S(1)} %pad_maximum_fusion.1.refs_1_, bf16[192,3072]{1,0:T(8,128)(2,1)} %collective-permute-done.2.refs_2_, ...), custom_call_target="tpu_custom_call" | custom-call | flops 1207959552 | bytes 19660800 | tf_op jit(solution)/shard_map/pallas_call | solution.py:86
  329.7 4.1 %all-to-all-start.8 = ((bf16[8,8,3072]{2,1,0:T(8,128)(2,1)}), bf16[8,8,3072]{2,1,0:T(8,128)(2,1)}, u32[]{:S(2)}, u32[]{:S(2)}) async-start(bf16[8,8,3072]{2,1,0:T(8,128)(2,1)} %bitcast.61), calls=%async_computation.8 | async-start | bytes 786432 | tf_op jit(solution)/shard_map/all_to_all | solution.py:178
  333.8 1.3 collective-permute-start
  336.3 11.2 %all-to-all-done.8 = bf16[8,8,3072]{2,1,0:T(8,128)(2,1)} async-done(((bf16[8,8,3072]{2,1,0:T(8,128)(2,1)}), bf16[8,8,3072]{2,1,0:T(8,128)(2,1)}, u32[]{:S(2)}, u32[]{:S(2)}) %all-to-all-start.8) | async-done | bytes 393248 | tf_op jit(solution)/shard_map/all_to_all | solution.py:178
  347.5 1.1 convert_reduce_fusion.1
  350.1 5.0 %collective-permute-start.18 = (bf16[8,3200]{1,0:T(8,128)(2,1)S(1)}, bf16[8,3200]{1,0:T(8,128)(2,1)S(1)}, u32[]{:S(2)}, u32[]{:S(2)}) collective-permute-start(bf16[8,3200]{1,0:T(8,128)(2,1)S(1)} %pad_maximum_fusion.5), channel_id=1, source_target_pairs={{0,64},{64,128},{128,192},{1,65},{65,129},{129,193},{2,66},{66,130... | collective-permute-start | bytes 153608 | tf_op jit(solution)/shard_map/ppermute | solution.py:30
  355.1 1.2 collective-permute-done.18
  356.3 15.1 %all_to_all.59 = bf16[8,8,3072]{2,1,0:T(8,128)(2,1)S(1)} all-to-all(bf16[8,8,3072]{2,1,0:T(8,128)(2,1)S(1)} %broadcast_in_dim.33), channel_id=1, replica_groups=mesh['zh'=2,'core'=2,'xh'=2,'xl'=2,'yh'=2,'yl'=2,'z'=4] {'xh','z'}, dimensions={0} | all-to-all | bytes 786432 | tf_op jit(solution)/shard_map/all_to_all | solution.py:36
  371.4 9.1 %shard_map.107 = bf16[64,3072]{1,0:T(8,128)(2,1)S(1)} custom-call(bf16[64,3072]{1,0:T(8,128)(2,1)S(1)} %bitcast.59, f32[3,3072]{1,0:T(4,128)S(1)} %reshape.84.mod_ref, bf16[192,3072]{1,0:T(8,128)(2,1)S(1)} %pad_maximum_fusion.refs_0_, bf16[192,3072]{1,0:T(8,128)(2,1)S(1)} %pad_maximum_fusion.1.refs_1_, bf16[192,3072]{1,0:T(8,128)(2,1)} %collective-permute-done.2.refs_2_, ...), custom_call_target="tpu_custom_call" | custom-call | flops 1207959552 | bytes 19660800 | tf_op jit(solution)/shard_map/pallas_call | solution.py:86
  381.3 3.6 all-to-all-start.10
  385.6 1.3 collective-permute-start.20
  387.7 12.1 %all-to-all-done.10 = bf16[8,8,3072]{2,1,0:T(8,128)(2,1)S(1)} async-done(((bf16[8,8,3072]{2,1,0:T(8,128)(2,1)}), bf16[8,8,3072]{2,1,0:T(8,128)(2,1)S(1)}, u32[]{:S(2)}, u32[]{:S(2)}) %all-to-all-start.10) | async-done | bytes 393248 | tf_op jit(solution)/shard_map/all_to_all | solution.py:178
  400.6 4.1 %collective-permute-start.22 = (bf16[8,3200]{1,0:T(8,128)(2,1)S(1)}, bf16[8,3200]{1,0:T(8,128)(2,1)S(1)}, u32[]{:S(2)}, u32[]{:S(2)}) collective-permute-start(bf16[8,3200]{1,0:T(8,128)(2,1)S(1)} %pad_maximum_fusion.6), channel_id=1, source_target_pairs={{0,64},{64,128},{128,192},{1,65},{65,129},{129,193},{2,66},{66,130... | collective-permute-start | bytes 153608 | tf_op jit(solution)/shard_map/ppermute | solution.py:30
  404.8 1.2 collective-permute-done.22
  (92 shorter events, 21.8 us)
Async XLA Ops:
  0.6 120.2 %copy-start = (bf16[1,144,3584]{2,1,0:T(8,128)(2,1)S(1)}, bf16[1,144,3584]{2,1,0:T(8,128)(2,1)}, u32[]{:S(2)}) copy-start(bf16[1,144,3584]{2,1,0:T(8,128)(2,1)} %param.15) | copy-start | bytes 3096580
  2.6 27.4 %collective-permute-start.5 = (bf16[192,3072]{1,0:T(8,128)(2,1)S(1)}, bf16[192,3072]{1,0:T(8,128)(2,1)}, u32[]{:S(2)}, u32[]{:S(2)}) collective-permute-start(bf16[192,3072]{1,0:T(8,128)(2,1)S(1)} %pad_maximum_fusion.1.refs_1_), channel_id=1, source_target_pairs={{12,0},{0,4},{4,8},{8,12},{13,1},{1,5},{5,9},{9,13},{14,2},{2,6},{... | collective-permute-start | bytes 3538952 | tf_op jit(solution)/shard_map/ppermute | solution.py:26
  4.8 56.1 %copy-start.9 = (bf16[8,3584]{1,0:T(8,128)(2,1)S(1)}, bf16[8,3584]{1,0:T(8,128)(2,1)}, u32[]{:S(2)}) copy-start(bf16[8,3584]{1,0:T(8,128)(2,1)} %param.13) | copy-start | bytes 172036
  4.9 29.4 %collective-permute-start.4 = (bf16[192,3072]{1,0:T(8,128)(2,1)S(1)}, bf16[192,3072]{1,0:T(8,128)(2,1)}, u32[]{:S(2)}, u32[]{:S(2)}) collective-permute-start(bf16[192,3072]{1,0:T(8,128)(2,1)S(1)} %pad_maximum_fusion.refs_0_), channel_id=1, source_target_pairs={{4,0},{8,4},{12,8},{0,12},{5,1},{9,5},{13,9},{1,13},{6,2},{10,6},{... | collective-permute-start | bytes 3538952 | tf_op jit(solution)/shard_map/ppermute | solution.py:26
  6.4 50.2 %collective-permute-start.6 = (bf16[192,3072]{1,0:T(8,128)(2,1)S(1)}, bf16[192,3072]{1,0:T(8,128)(2,1)}, u32[]{:S(2)}, u32[]{:S(2)}) collective-permute-start(bf16[192,3072]{1,0:T(8,128)(2,1)S(1)} %pad_maximum_fusion.1.refs_1_), channel_id=1, source_target_pairs={{4,0},{8,4},{12,8},{0,12},{5,1},{9,5},{13,9},{1,13},{6,2},{10,6},{... | collective-permute-start | bytes 3538952 | tf_op jit(solution)/shard_map/ppermute | solution.py:26
  7.8 50.2 %collective-permute-start.7 = (bf16[192,3072]{1,0:T(8,128)(2,1)S(1)}, bf16[192,3072]{1,0:T(8,128)(2,1)}, u32[]{:S(2)}, u32[]{:S(2)}) collective-permute-start(bf16[192,3072]{1,0:T(8,128)(2,1)S(1)} %pad_maximum_fusion.refs_0_), channel_id=1, source_target_pairs={{12,0},{0,4},{4,8},{8,12},{13,1},{1,5},{5,9},{9,13},{14,2},{2,6},{... | collective-permute-start | bytes 3538952 | tf_op jit(solution)/shard_map/ppermute | solution.py:26
  7.9 107.0 %collective-permute-start.3 = (bf16[192,3072]{1,0:T(8,128)(2,1)S(1)}, bf16[192,3072]{1,0:T(8,128)(2,1)}, u32[]{:S(2)}, u32[]{:S(2)}) collective-permute-start(bf16[192,3072]{1,0:T(8,128)(2,1)S(1)} %pad_maximum_fusion.1.refs_1_), channel_id=1, source_target_pairs={{48,0},{0,16},{16,32},{32,48},{49,1},{1,17},{17,33},{33,49},{50,2}... | collective-permute-start | bytes 3538952 | tf_op jit(solution)/shard_map/ppermute | solution.py:26
  30.0 85.5 %collective-permute-start.2 = (bf16[192,3072]{1,0:T(8,128)(2,1)S(1)}, bf16[192,3072]{1,0:T(8,128)(2,1)}, u32[]{:S(2)}, u32[]{:S(2)}) collective-permute-start(bf16[192,3072]{1,0:T(8,128)(2,1)S(1)} %pad_maximum_fusion.refs_0_), channel_id=1, source_target_pairs={{16,0},{32,16},{48,32},{0,48},{17,1},{33,17},{49,33},{1,49},{18,2}... | collective-permute-start | bytes 3538952 | tf_op jit(solution)/shard_map/ppermute | solution.py:26
  34.3 82.2 %collective-permute-start.11 = (bf16[192,3072]{1,0:T(8,128)(2,1)}, bf16[192,3072]{1,0:T(8,128)(2,1)}, u32[]{:S(2)}, u32[]{:S(2)}) collective-permute-start(bf16[192,3072]{1,0:T(8,128)(2,1)} %collective-permute-done.5.refs_5_), channel_id=1, source_target_pairs={{12,0},{0,4},{4,8},{8,12},{13,1},{1,5},{5,9},{9,13},{14,2},{2,6},{... | collective-permute-start | bytes 3538952 | tf_op jit(solution)/shard_map/ppermute | solution.py:26
  56.6 61.5 %collective-permute-start.9 = (bf16[192,3072]{1,0:T(8,128)(2,1)}, bf16[192,3072]{1,0:T(8,128)(2,1)}, u32[]{:S(2)}, u32[]{:S(2)}) collective-permute-start(bf16[192,3072]{1,0:T(8,128)(2,1)} %collective-permute-done.5.refs_5_), channel_id=1, source_target_pairs={{48,0},{0,16},{16,32},{32,48},{49,1},{1,17},{17,33},{33,49},{50,2}... | collective-permute-start | bytes 3538952 | tf_op jit(solution)/shard_map/ppermute | solution.py:26
  58.1 60.1 %collective-permute-start.10 = (bf16[192,3072]{1,0:T(8,128)(2,1)}, bf16[192,3072]{1,0:T(8,128)(2,1)}, u32[]{:S(2)}, u32[]{:S(2)}) collective-permute-start(bf16[192,3072]{1,0:T(8,128)(2,1)} %collective-permute-done.4.refs_4_), channel_id=1, source_target_pairs={{4,0},{8,4},{12,8},{0,12},{5,1},{9,5},{13,9},{1,13},{6,2},{10,6},{... | collective-permute-start | bytes 3538952 | tf_op jit(solution)/shard_map/ppermute | solution.py:26
  90.3 104.1 %copy-start.7 = (bf16[1,8,3072]{2,1,0:T(8,128)(2,1)S(1)}, bf16[1,8,3072]{2,1,0:T(8,128)(2,1)}, u32[]{:S(2)}) copy-start(bf16[1,8,3072]{2,1,0:T(8,128)(2,1)} %param.9) | copy-start | bytes 147460
  91.1 21.5 %all-to-all-start.1 = ((f32[16,28,128]{2,1,0:T(8,128)}), f32[16,28,128]{2,1,0:T(8,128)}, u32[]{:S(2)}, u32[]{:S(2)}) async-start(f32[16,28,128]{2,1,0:T(8,128)} %broadcast_in_dim.26), calls=%async_computation.1 | async-start | bytes 524288 | tf_op jit(solution)/shard_map/all_to_all | solution.py:36
  114.9 98.0 %collective-permute-start.8 = (bf16[192,3072]{1,0:T(8,128)(2,1)}, bf16[192,3072]{1,0:T(8,128)(2,1)}, u32[]{:S(2)}, u32[]{:S(2)}) collective-permute-start(bf16[192,3072]{1,0:T(8,128)(2,1)} %collective-permute-done.4.refs_4_), channel_id=1, source_target_pairs={{16,0},{32,16},{48,32},{0,48},{17,1},{33,17},{49,33},{1,49},{18,2}... | collective-permute-start | bytes 3538952 | tf_op jit(solution)/shard_map/ppermute | solution.py:26
  115.5 97.5 %collective-permute-start.13 = (bf16[192,3072]{1,0:T(8,128)(2,1)}, bf16[192,3072]{1,0:T(8,128)(2,1)}, u32[]{:S(2)}, u32[]{:S(2)}) collective-permute-start(bf16[192,3072]{1,0:T(8,128)(2,1)} %collective-permute-done.6.refs_6_), channel_id=1, source_target_pairs={{48,0},{0,16},{16,32},{32,48},{49,1},{1,17},{17,33},{33,49},{50,2}... | collective-permute-start | bytes 3538952 | tf_op jit(solution)/shard_map/ppermute | solution.py:26
  116.4 96.5 %collective-permute-start.12 = (bf16[192,3072]{1,0:T(8,128)(2,1)}, bf16[192,3072]{1,0:T(8,128)(2,1)}, u32[]{:S(2)}, u32[]{:S(2)}) collective-permute-start(bf16[192,3072]{1,0:T(8,128)(2,1)} %collective-permute-done.7.refs_7_), channel_id=1, source_target_pairs={{16,0},{32,16},{48,32},{0,48},{17,1},{33,17},{49,33},{1,49},{18,2}... | collective-permute-start | bytes 3538952 | tf_op jit(solution)/shard_map/ppermute | solution.py:26
  118.1 94.8 %collective-permute-start.15 = (bf16[192,3072]{1,0:T(8,128)(2,1)}, bf16[192,3072]{1,0:T(8,128)(2,1)}, u32[]{:S(2)}, u32[]{:S(2)}) collective-permute-start(bf16[192,3072]{1,0:T(8,128)(2,1)} %collective-permute-done.11.refs_11_), channel_id=1, source_target_pairs={{48,0},{0,16},{16,32},{32,48},{49,1},{1,17},{17,33},{33,49},{50,2}... | collective-permute-start | bytes 3538952 | tf_op jit(solution)/shard_map/ppermute | solution.py:26
  118.2 94.8 %collective-permute-start.14 = (bf16[192,3072]{1,0:T(8,128)(2,1)}, bf16[192,3072]{1,0:T(8,128)(2,1)}, u32[]{:S(2)}, u32[]{:S(2)}) collective-permute-start(bf16[192,3072]{1,0:T(8,128)(2,1)} %collective-permute-done.10.refs_10_), channel_id=1, source_target_pairs={{16,0},{32,16},{48,32},{0,48},{17,1},{33,17},{49,33},{1,49},{18,2}... | collective-permute-start | bytes 3538952 | tf_op jit(solution)/shard_map/ppermute | solution.py:26
  195.2 17.7 %all-to-all-start.3 = ((bf16[8,8,3072]{2,1,0:T(8,128)(2,1)}), bf16[8,8,3072]{2,1,0:T(8,128)(2,1)}, u32[]{:S(2)}, u32[]{:S(2)}) async-start(bf16[8,8,3072]{2,1,0:T(8,128)(2,1)} %broadcast_in_dim.29), calls=%async_computation.3 | async-start | bytes 786432 | tf_op jit(solution)/shard_map/all_to_all | solution.py:36
  212.9 15.7 %copy-start.10 = (s32[1,8]{1,0:T(1,128)S(1)}, s32[1,8]{1,0:T(1,128)}, u32[]{:S(2)}) copy-start(s32[1,8]{1,0:T(1,128)} %param.10) | copy-start | bytes 100
  223.1 0.8 copy-start.4
  223.8 15.1 %all-to-all-start.4 = ((bf16[8,8,3072]{2,1,0:T(8,128)(2,1)}), bf16[8,8,3072]{2,1,0:T(8,128)(2,1)}, u32[]{:S(2)}, u32[]{:S(2)}) async-start(bf16[8,8,3072]{2,1,0:T(8,128)(2,1)} %bitcast.62), calls=%async_computation.4 | async-start | bytes 786432 | tf_op jit(solution)/shard_map/all_to_all | solution.py:178
  241.5 10.5 %collective-permute-start.16 = (bf16[8,3200]{1,0:T(8,128)(2,1)}, bf16[8,3200]{1,0:T(8,128)(2,1)S(1)}, u32[]{:S(2)}, u32[]{:S(2)}) collective-permute-start(bf16[8,3200]{1,0:T(8,128)(2,1)} %pad_maximum_fusion.3), channel_id=1, source_target_pairs={{0,64},{64,128},{128,192},{192,0},{1,65},{65,129},{129,193},{193,1... | collective-permute-start | bytes 153608 | tf_op jit(solution)/shard_map/ppermute | solution.py:30
  252.0 0.6 copy-start.5
  276.5 0.8 copy-start.2
  277.2 15.1 %all-to-all-start.6 = ((bf16[8,8,3072]{2,1,0:T(8,128)(2,1)}), bf16[8,8,3072]{2,1,0:T(8,128)(2,1)}, u32[]{:S(2)}, u32[]{:S(2)}) async-start(bf16[8,8,3072]{2,1,0:T(8,128)(2,1)} %bitcast.60), calls=%async_computation.6 | async-start | bytes 786432 | tf_op jit(solution)/shard_map/all_to_all | solution.py:178
  282.5 21.1 %collective-permute-start.1 = (bf16[8,3200]{1,0:T(8,128)(2,1)}, bf16[8,3200]{1,0:T(8,128)(2,1)}, u32[]{:S(2)}, u32[]{:S(2)}) collective-permute-start(bf16[8,3200]{1,0:T(8,128)(2,1)} %get-tuple-element.9), channel_id=1, source_target_pairs={{64,0},{65,1},{66,2},{67,3},{68,4},{69,5},{70,6},{71,7},{72,8},{73... | collective-permute-start | bytes 153608 | tf_op jit(solution)/shard_map/ppermute | solution.py:30
  294.8 10.0 %collective-permute-start.17 = (bf16[8,3200]{1,0:T(8,128)(2,1)S(1)}, bf16[8,3200]{1,0:T(8,128)(2,1)S(1)}, u32[]{:S(2)}, u32[]{:S(2)}) collective-permute-start(bf16[8,3200]{1,0:T(8,128)(2,1)S(1)} %pad_maximum_fusion.4), channel_id=1, source_target_pairs={{0,64},{64,128},{128,192},{1,65},{65,129},{129,193},{2,66},{66,130... | collective-permute-start | bytes 153608 | tf_op jit(solution)/shard_map/ppermute | solution.py:30
  329.0 0.8 copy-start.3
  329.7 17.8 %all-to-all-start.8 = ((bf16[8,8,3072]{2,1,0:T(8,128)(2,1)}), bf16[8,8,3072]{2,1,0:T(8,128)(2,1)}, u32[]{:S(2)}, u32[]{:S(2)}) async-start(bf16[8,8,3072]{2,1,0:T(8,128)(2,1)} %bitcast.61), calls=%async_computation.8 | async-start | bytes 786432 | tf_op jit(solution)/shard_map/all_to_all | solution.py:178
  333.8 21.2 %collective-permute-start = (bf16[8,3200]{1,0:T(8,128)(2,1)}, bf16[8,3200]{1,0:T(8,128)(2,1)}, u32[]{:S(2)}, u32[]{:S(2)}) collective-permute-start(bf16[8,3200]{1,0:T(8,128)(2,1)} %get-tuple-element.9), channel_id=1, source_target_pairs={{128,0},{129,1},{130,2},{131,3},{132,4},{133,5},{134,6},{135,7},{1... | collective-permute-start | bytes 153608 | tf_op jit(solution)/shard_map/ppermute | solution.py:30
  349.3 6.9 %copy-start.8 = (bf16[8,3072]{1,0:T(8,128)(2,1)}, bf16[8,3072]{1,0:T(8,128)(2,1)S(1)}, u32[]{:S(2)}) copy-start(bf16[8,3072]{1,0:T(8,128)(2,1)S(1)} %add_convert_fusion.1) | copy-start | bytes 147460
  350.1 6.2 %collective-permute-start.18 = (bf16[8,3200]{1,0:T(8,128)(2,1)S(1)}, bf16[8,3200]{1,0:T(8,128)(2,1)S(1)}, u32[]{:S(2)}, u32[]{:S(2)}) collective-permute-start(bf16[8,3200]{1,0:T(8,128)(2,1)S(1)} %pad_maximum_fusion.5), channel_id=1, source_target_pairs={{0,64},{64,128},{128,192},{1,65},{65,129},{129,193},{2,66},{66,130... | collective-permute-start | bytes 153608 | tf_op jit(solution)/shard_map/ppermute | solution.py:30
  380.5 0.8 copy-start.1
  381.3 18.6 %copy-start.6 = (bf16[8,3200]{1,0:T(8,128)(2,1)S(1)}, bf16[8,3200]{1,0:T(8,128)(2,1)}, u32[]{:S(2)}) copy-start(bf16[8,3200]{1,0:T(8,128)(2,1)} %copy-done.5) | copy-start | bytes 153604
  381.3 18.5 %all-to-all-start.10 = ((bf16[8,8,3072]{2,1,0:T(8,128)(2,1)}), bf16[8,8,3072]{2,1,0:T(8,128)(2,1)S(1)}, u32[]{:S(2)}, u32[]{:S(2)}) async-start(bf16[8,8,3072]{2,1,0:T(8,128)(2,1)} %bitcast.58), calls=%async_computation.10 | async-start | bytes 786432 | tf_op jit(solution)/shard_map/all_to_all | solution.py:178
  384.9 19.9 %collective-permute-start.21 = (bf16[8,3200]{1,0:T(8,128)(2,1)}, bf16[8,3200]{1,0:T(8,128)(2,1)S(1)}, u32[]{:S(2)}, u32[]{:S(2)}) collective-permute-start(bf16[8,3200]{1,0:T(8,128)(2,1)} %get-tuple-element.9), channel_id=1, source_target_pairs={{192,0},{193,1},{194,2},{195,3},{196,4},{197,5},{198,6},{199,7},{2... | collective-permute-start | bytes 153608 | tf_op jit(solution)/shard_map/ppermute | solution.py:30
  385.6 14.3 %collective-permute-start.20 = (bf16[8,3072]{1,0:T(8,128)(2,1)S(1)}, bf16[8,3072]{1,0:T(8,128)(2,1)S(1)}, u32[]{:S(2)}, u32[]{:S(2)}) collective-permute-start(bf16[8,3072]{1,0:T(8,128)(2,1)S(1)} %add_convert_fusion.2), channel_id=1, source_target_pairs={{192,64},{193,65},{194,66},{195,67},{196,68},{197,69},{198,70},{19... | collective-permute-start | bytes 147464 | tf_op jit(solution)/shard_map/ppermute | solution.py:30
  386.9 13.0 %collective-permute-start.19 = (bf16[8,3072]{1,0:T(8,128)(2,1)}, bf16[8,3072]{1,0:T(8,128)(2,1)S(1)}, u32[]{:S(2)}, u32[]{:S(2)}) collective-permute-start(bf16[8,3072]{1,0:T(8,128)(2,1)} %copy-done.8), channel_id=1, source_target_pairs={{192,128},{193,129},{194,130},{195,131},{196,132},{197,133},{198,1... | collective-permute-start | bytes 147464 | tf_op jit(solution)/shard_map/ppermute | solution.py:30
  400.6 5.3 %collective-permute-start.22 = (bf16[8,3200]{1,0:T(8,128)(2,1)S(1)}, bf16[8,3200]{1,0:T(8,128)(2,1)S(1)}, u32[]{:S(2)}, u32[]{:S(2)}) collective-permute-start(bf16[8,3200]{1,0:T(8,128)(2,1)S(1)} %pad_maximum_fusion.6), channel_id=1, source_target_pairs={{0,64},{64,128},{128,192},{1,65},{65,129},{129,193},{2,66},{66,130... | collective-permute-start | bytes 153608 | tf_op jit(solution)/shard_map/ppermute | solution.py:30

commit v2 on v1

--- a/solution.py
+++ b/solution.py
@@ -11,11 +11,12 @@
 f32 = jnp.float32
 bf16 = jnp.bfloat16
 
-SIZES = {"zh": 2, "core": 2, "xh": 2, "xl": 2, "yh": 2, "yl": 2, "z": 4}
+SIZES = {"zh": 2, "core": 2, "xh": 2, "xl": 2, "yh": 2, "yl": 2, "zc": 2, "zf": 2}
 SECTION = ("zh", "core")
-TP = ("xh", "xl", "yh", "yl", "z")
+TP = ("xh", "xl", "yh", "yl", "zc", "zf")
 PLANE = ("xh", "xl", "yh", "yl")
-GROUP = ("xh", "z")
+LINE = ("zc", "zf")
+GROUP = ("xh",) + LINE
 GROUP_SIZE = 8
 SECTIONS = 4
 LANES = 128
@@ -27,7 +28,14 @@
 
 
 def between_sections(block, edges):
-    return lax.ppermute(block, SECTION, edges)
+    route = [
+        (2 * start + half, 2 * end + (half ^ flip)) for start, end, flip in edges for half in (0, 1)
+    ]
+    return lax.ppermute(block, SECTION + ("zc",), route)
+
+
+def after(value, *earlier):
+    return lax.optimization_barrier((value,) + earlier)[0]
 
 
 def exchange(block, axes):
@@ -38,7 +46,7 @@
 
 def ffn_kernel(pieces, half, x_ref, mod_ref, *refs):
     weights = refs[:pieces]
-    out_ref, up, down, inputs, hidden, sem = refs[pieces:]
+    out_ref, up, down, inputs, hidden, acc, sem = refs[pieces:]
     lifts, drops = [], []
     for i, w in enumerate(weights):
         rows = pl.ds(i * half, half)
@@ -69,12 +77,22 @@
             preferred_element_type=f32,
         )
         hidden[:, at : at + step] = jax.nn.gelu(raised, approximate=True).astype(bf16)
-    for copy in drops:
-        copy.wait()
-    for at in range(0, out_ref.shape[1], step):
-        out_ref[:, at : at + step] = jnp.dot(
-            hidden[...], down[:, at : at + step], preferred_element_type=f32
-        ).astype(bf16)
+    arrived = 0
+    for at in range(0, total, step):
+        while arrived * half < at + step:
+            drops[arrived].wait()
+            arrived += 1
+        for column in range(0, out_ref.shape[1], step):
+            columns = slice(column, column + step)
+            term = jnp.dot(
+                hidden[:, at : at + step], down[at : at + step, columns], preferred_element_type=f32
+            )
+            if at:
+                term = acc[:, columns] + term
+            if at + step < total:
+                acc[:, columns] = term
+            else:
+                out_ref[:, columns] = term.astype(bf16)
 
 
 def ffn(tokens, mod, weights):
@@ -93,6 +111,7 @@
             pltpu.VMEM((total, breadth), bf16),
             pltpu.VMEM((rows, breadth), bf16),
             pltpu.VMEM((rows, total), bf16),
+            pltpu.VMEM((rows, breadth), f32),
             pltpu.SemaphoreType.DMA((2, pieces)),
         ],
         compiler_params=pltpu.CompilerParams(vmem_limit_bytes=40 * 1024 * 1024),
@@ -104,38 +123,55 @@
     )(tokens, mod, *weights)
 
 
-def spread_weights(up, down):
+def close_kernel(parts_ref, waiting_ref, gate_ref, out_ref):
+    breadth = parts_ref.shape[2]
+    result = parts_ref[0].astype(f32)
+    for i in range(1, parts_ref.shape[0]):
+        result += parts_ref[i].astype(f32)
+    mask = waiting_ref[:, breadth:]
+    kept = mask[:, :1].astype(f32)
+    values = waiting_ref[:, :breadth].astype(f32)
+    out_ref[:, :breadth] = (values + kept * gate_ref[...] * result).astype(bf16)
+    out_ref[:, breadth:] = mask
+
+
+def close(parts, waiting, gate):
+    whole = pl.BlockSpec(memory_space=pltpu.VMEM)
+    return pl.pallas_call(
+        close_kernel,
+        out_shape=jax.ShapeDtypeStruct(waiting.shape, waiting.dtype),
+        in_specs=[whole] * 3,
+        out_specs=whole,
+        cost_estimate=pl.CostEstimate(
+            flops=parts.size, bytes_accessed=2 * parts.size, transcendentals=0
+        ),
+    )(parts, waiting, gate)
+
+
+def set_out(up, down, prompt_embeddings, prompt_tally, adaptive_norm_weights, waiting):
     middle = up.shape[0] // 2
     first = jnp.concatenate([up[:middle], down[:middle]], axis=0)
     second = jnp.concatenate([up[middle:], down[middle:]], axis=0)
-    xa = from_neighbour(first, "x", 1)
-    xb = from_neighbour(second, "x", -1)
-    yp_first = from_neighbour(first, "y", 1)
-    ym_second = from_neighbour(second, "y", -1)
-    yp_second = from_neighbour(second, "y", 1)
-    ym_first = from_neighbour(first, "y", -1)
-    xa_yp = from_neighbour(yp_first, "x", 1)
-    xb_ym = from_neighbour(ym_second, "x", -1)
-    y2_first = from_neighbour(yp_first, "y", 1)
-    y2_second = from_neighbour(ym_second, "y", -1)
-    xa_ym = from_neighbour(ym_first, "x", 1)
-    xb_yp = from_neighbour(yp_second, "x", -1)
-    xa_y2 = from_neighbour(y2_first, "x", 1)
-    xb_y2 = from_neighbour(y2_second, "x", -1)
-    return [
-        first, second, xa, xb, yp_first, ym_second, yp_second, ym_first,
-        xa_yp, xb_ym, y2_first, y2_second, xa_ym, xb_yp, xa_y2, xb_y2,
-    ]
-
-
-def condition(prompt_embeddings, prompt_tally, adaptive_norm_weights):
     count_rows, encoded = prompt_embeddings.shape
     first_row = lax.axis_index(SECTION + TP) * count_rows
     keep = (first_row + lax.iota(jnp.int32, count_rows) < prompt_tally[0]).astype(bf16)
     partial = jnp.dot(keep[None, :], prompt_embeddings, preferred_element_type=f32)
     partial = partial.reshape(encoded // LANES, LANES)
     partial = jnp.sum(exchange(partial, PLANE), axis=0)
-    pooled = jnp.sum(exchange(partial, ("zh", "core", "z")), axis=0)
+
+    first, second = after((first, second), partial)
+    yp_first = from_neighbour(first, "y", 1)
+    ym_second = from_neighbour(second, "y", -1)
+    xa = from_neighbour(first, "x", 1)
+    xb = from_neighbour(second, "x", -1)
+    yp_second = from_neighbour(second, "y", 1)
+    ym_first = from_neighbour(first, "y", -1)
+
+    pooled = jnp.sum(exchange(partial, SECTION + LINE), axis=0)
+    yp_first, ym_second = after((yp_first, ym_second), pooled)
+    xa_yp = from_neighbour(yp_first, "x", 1)
+    xb_ym = from_neighbour(ym_second, "x", -1)
+
     pooled = pooled / prompt_tally[0].astype(f32)
     normed = pooled * lax.rsqrt(jnp.mean(pooled * pooled) + 1e-06)
     cond = jax.nn.silu(normed).astype(bf16).reshape(encoded)
@@ -143,8 +179,31 @@
     columns = local.shape[0]
     rows = -(-columns // LANES)
     local = jnp.pad(local, (0, rows * LANES - columns)).reshape(rows, LANES)
-    modes = exchange(local, TP)
-    return modes.reshape(modes.shape[0], rows * LANES)[:, :columns].reshape(3, -1)
+    line = exchange(local, LINE)
+
+    yp_first, ym_second, yp_second, ym_first = after(
+        (yp_first, ym_second, yp_second, ym_first), line
+    )
+    y2_first = from_neighbour(yp_first, "y", 1)
+    y2_second = from_neighbour(ym_second, "y", -1)
+    xa_ym = from_neighbour(ym_first, "x", 1)
+    xb_yp = from_neighbour(yp_second, "x", -1)
+    xa_y2 = from_neighbour(y2_first, "x", 1)
+    xb_y2 = from_neighbour(y2_second, "x", -1)
+
+    modes = exchange(line, PLANE)
+    modes = modes.reshape(-1, rows * LANES)[:, :columns].reshape(3, -1)
+
+    waiting = after(waiting, line)
+    mine = exchange(waiting, LINE)
+    theirs = lax.ppermute(mine, "xh", [(0, 1), (1, 0)])
+    upper = lax.axis_index("xh") == 1
+    gathered = jnp.stack([jnp.where(upper, theirs, mine), jnp.where(upper, mine, theirs)])
+    pieces = [
+        first, second, xa, xb, yp_first, ym_second, yp_second, ym_first,
+        xa_yp, xb_ym, y2_first, y2_second, xa_ym, xb_yp, xa_y2, xb_y2,
+    ]
+    return modes, gathered, pieces
 
 
 def per_device(
@@ -168,33 +227,37 @@
 
     arriving = with_mask(arriving_tiles[0], arriving_region[0])
     waiting = with_mask(travelling_inputs[0], travelling_region[0])
-    entering = [arriving] + [between_sections(arriving, [(s, 0)]) for s in range(1, SECTIONS)]
-    mod = condition(prompt_embeddings, prompt_tally, adaptive_norm_weights[0])
-    weights = spread_weights(expansion_weights[0], contraction_weights[0])
-    finished = None
+    last = SECTIONS - 1
+    entering = [arriving]
+    for section in range(1, SECTIONS):
+        entering.append(between_sections(arriving, [(section, 0, 0)]))
+    mod, gathered, weights = set_out(
+        expansion_weights[0],
+        contraction_weights[0],
+        prompt_embeddings,
+        prompt_tally,
+        adaptive_norm_weights[0],
+        travelling_inputs[0],
+    )
+    finished = []
     for tick in range(SECTIONS):
-        gathered = exchange(waiting[:, :breadth], GROUP)
+        if tick:
+            gathered = exchange(waiting[:, :breadth], GROUP)
         partial = ffn(gathered.reshape(GROUP_SIZE * tokens, breadth), mod, weights)
         parts = lax.all_to_all(partial.reshape(GROUP_SIZE, tokens, breadth), GROUP, 0, 0)
-        result = jnp.sum(parts.astype(f32), axis=0)
-        mask = waiting[:, breadth:]
-        produced = (
-            waiting[:, :breadth].astype(f32) + mask[:, :1].astype(f32) * mod[2][None] * result
-        ).astype(bf16)
-        produced = jnp.concatenate([produced, mask], axis=1)
-        edges = [(s, s + 1) for s in range(SECTIONS - 1)]
-        if tick == 0:
-            moved = between_sections(produced, edges + [(SECTIONS - 1, 0)])
-            finished = moved
+        produced = close(parts, waiting, mod[2:])
+        if tick < last:
+            moved = between_sections(produced, [(0, 1, 0), (1, 2, 1), (2, 3, 0)])
+            flip = int(tick >= 2)
+            finished.append(between_sections(produced[:, :breadth], [(last, tick, flip)]))
         else:
-            moved = between_sections(produced, edges)
-            if tick < SECTIONS - 1:
-                left = between_sections(produced[:, :breadth], [(SECTIONS - 1, tick)])
-            else:
-                left = produced[:, :breadth]
-            finished = jnp.where(section_id == tick, left, finished[:, :breadth])
+            moved = between_sections(produced, [(0, 1, 0), (1, 2, 0), (2, 3, 1)])
+            finished.append(between_sections(produced[:, :breadth], [(last, last, 1)]))
         waiting = jnp.where(is_first, entering[tick], moved)
-    return finished[None], waiting[None, :, :breadth]
+    done = finished[last]
+    for tick in range(last):
+        done = jnp.where(section_id == tick, finished[tick], done)
+    return done[None], waiting[None, :, :breadth]
 
 
 def solution(mesh):

time: 408 us -> 403 us (0.988)
  blocking collectives: 145 us -> 59 us
  waiting for transfers between devices: 103 us -> 160 us
  local copies, waits for them, and re-layouts: 10 us -> 29.7 us
  other arithmetic: 14.9 us -> 7.33 us
  Pallas kernels: 37.5 us -> 45 us
    all_to_all x5, blocking collectives: 145 us -> 59 us  [exchange(): return lax.all_to_all(copies, axes, 0, 0)]
    all_to_all x2 -> x3, waiting for transfers between devices: 20.2 us -> 51.2 us  [exchange(): return lax.all_to_all(copies, axes, 0, 0)]
    ppermute x14, waiting for transfers between devices: 42.7 us -> 66.1 us  [from_neighbour(): return lax.ppermute(block, (axis + 'h', axis + 'l'), route)]
    unnamed x23 -> x75, local copies, waits for them, and re-layouts: 4.4 us -> 20.6 us
    all_to_all x2 -> x3, starting transfers between devices: 18.1 us -> 25.4 us  [exchange(): return lax.all_to_all(copies, axes, 0, 0)]
    pallas_call x0 -> x4, Pallas kernels: none -> 6.92 us  [close(): pl.pallas_call(close_kernel, out_shape=jax.ShapeDtypeStruct(waiting.shape...]
    ppermute x14, starting transfers between devices: 20.8 us -> 15.9 us  [from_neighbour(): return lax.ppermute(block, (axis + 'h', axis + 'l'), route)]
    reduce_sum x7 -> x3, other arithmetic: 5.79 us -> 1.61 us  [the longest x1 0.97 us: set_out(): pooled = jnp.sum(exchange(partial, SECTION + LINE), axis=0)]
  transfers between devices with their start and end apart: 29 -> 33, of which waited for: 12 -> 15; matrix products, arithmetic and copies ran while one was open for 4% -> 4% of each run, Pallas kernels for 0% -> 1%
where the time goes in v2:
time: 403 us; the launch traced here: 399 us
  waiting for transfers between devices  160 us (40%)
  starting transfers between devices  93.5 us (23%)
  blocking collectives  59 us (15%)
  Pallas kernels  45 us (11%)
  local copies, waits for them, and re-layouts  29.7 us (7%)
  other arithmetic  7.33 us (2%)
    ppermute x14, waiting for transfers between devices, from_neighbour(): return lax.ppermute(block, (axis + 'h', axis + 'l'), route)  66.1 us
    all_to_all x5, blocking collectives, exchange(): return lax.all_to_all(copies, axes, 0, 0)  59 us
    all_to_all x3, waiting for transfers between devices, exchange(): return lax.all_to_all(copies, axes, 0, 0)  51.2 us
    all_to_all x4, waiting for transfers between devices, per_device(): lax.all_to_all(partial.reshape(GROUP_SIZE, tokens, breadth), GROUP, 0, 0)  38.5 us
    pallas_call x4, Pallas kernels, ffn(): pl.pallas_call(functools.partial(ffn_kernel, pieces, half), out_shape=jax...  38 us
    ppermute x11, starting transfers between devices, between_sections(): return lax.ppermute(block, SECTION + ('zc',), route)  35.2 us
    all_to_all x3, starting transfers between devices, exchange(): return lax.all_to_all(copies, axes, 0, 0)  25.4 us
    unnamed x75, local copies, waits for them, and re-layouts  20.6 us
  transfers between devices with their start and end apart: 33, of which 15 were waited for; matrix products, arithmetic and copies ran while one was open for 4% of the time, Pallas kernels for 1%

profile of v2, /device:TPU:1, one launch (start us, length us, event | category | flops | bytes accessed | tf_op | source)
XLA Modules:
  0.0 398.9 jit_solution(18195756875657553509)
XLA Ops:
  3.1 7.6 %all-to-all-start = ((f32[16,28,128]{2,1,0:T(8,128)}), f32[16,28,128]{2,1,0:T(8,128)S(1)}, u32[]{:S(2)}, u32[]{:S(2)}) async-start(f32[16,28,128]{2,1,0:T(8,128)} %broadcast_in_dim.27), calls=%async_computation | async-start | bytes 524288 | tf_op jit(solution)/shard_map/all_to_all | solution.py:44
  10.7 2.5 slice_bitcast_fusion
  13.2 5.0 %all-to-all-done = f32[16,28,128]{2,1,0:T(8,128)S(1)} async-done(((f32[16,28,128]{2,1,0:T(8,128)}), f32[16,28,128]{2,1,0:T(8,128)S(1)}, u32[]{:S(2)}, u32[]{:S(2)}) %all-to-all-start) | async-done | bytes 229408 | tf_op jit(solution)/shard_map/all_to_all | solution.py:44
  18.9 10.5 %all-to-all-start.1 = ((f32[16,28,128]{2,1,0:T(8,128)}), f32[16,28,128]{2,1,0:T(8,128)}, u32[]{:S(2)}, u32[]{:S(2)}) async-start(f32[16,28,128]{2,1,0:T(8,128)} %broadcast_in_dim.28), calls=%async_computation.1 | async-start | bytes 524288 | tf_op jit(solution)/shard_map/all_to_all | solution.py:44
  30.5 1.8 pad_maximum_fusion
  32.6 2.5 collective-permute-start.6
  35.1 1.4 collective-permute-start.7
  36.5 2.6 all-to-all-done.1
  41.8 8.7 %all_to_all.60 = f32[4,2,128]{2,1,0:T(2,128)S(1)} all-to-all(f32[4,2,128]{2,1,0:T(2,128)S(1)} %broadcast_in_dim.30), channel_id=1, replica_groups=mesh['zh'=2,'core'=2,'xh'=2,'xl'=2,'yh'=2,'yl'=2,'zc'=2,'zf'=2] {'zc','zf'}, dimensions={0} | all-to-all | bytes 8192 | tf_op jit(solution)/shard_map/all_to_all | solution.py:44
  50.5 8.1 %all_to_all.61 = bf16[4,8,3072]{2,1,0:T(8,128)(2,1)S(1)} all-to-all(bf16[4,8,3072]{2,1,0:T(8,128)(2,1)S(1)} %broadcast_in_dim.31), channel_id=1, replica_groups=mesh['zh'=2,'core'=2,'xh'=2,'xl'=2,'yh'=2,'yl'=2,'zc'=2,'zf'=2] {'zc','zf'}, dimensions={0} | all-to-all | bytes 393216 | tf_op jit(solution)/shard_map/all_to_all | solution.py:44
  59.6 25.6 %collective-permute-done.4.refs_4_ = bf16[192,3072]{1,0:T(8,128)(2,1)} collective-permute-done((bf16[192,3072]{1,0:T(8,128)(2,1)S(1)}, bf16[192,3072]{1,0:T(8,128)(2,1)}, u32[]{:S(2)}, u32[]{:S(2)}) %collective-permute-start.4) | collective-permute-done | bytes 1179680 | tf_op jit(solution)/shard_map/ppermute | solution.py:27
  86.7 2.0 collective-permute-start.8
  88.7 3.5 collective-permute-start.10
  92.2 19.3 %collective-permute-done.2.refs_2_ = bf16[192,3072]{1,0:T(8,128)(2,1)S(1)} collective-permute-done((bf16[192,3072]{1,0:T(8,128)(2,1)S(1)}, bf16[192,3072]{1,0:T(8,128)(2,1)S(1)}, u32[]{:S(2)}, u32[]{:S(2)}) %collective-permute-start.2) | collective-permute-done | bytes 1179680 | tf_op jit(solution)/shard_map/ppermute | solution.py:27
  114.3 2.0 collective-permute-start.12
  116.3 20.5 %collective-permute-done.8.refs_8_ = bf16[192,3072]{1,0:T(8,128)(2,1)S(1)} collective-permute-done((bf16[192,3072]{1,0:T(8,128)(2,1)}, bf16[192,3072]{1,0:T(8,128)(2,1)S(1)}, u32[]{:S(2)}, u32[]{:S(2)}) %collective-permute-start.8) | collective-permute-done | bytes 1179680 | tf_op jit(solution)/shard_map/ppermute | solution.py:27
  137.8 2.7 collective-permute-start.14
  141.2 7.3 %all-to-all-start.4 = ((f32[16,4,2,128]{3,2,1,0:T(2,128)}), f32[16,4,2,128]{3,2,1,0:T(2,128)S(1)}, u32[]{:S(2)}, u32[]{:S(2)}) async-start(f32[16,4,2,128]{3,2,1,0:T(2,128)} %broadcast_in_dim.32), calls=%async_computation.4 | async-start | bytes 131072 | tf_op jit(solution)/shard_map/all_to_all | solution.py:44
  148.4 43.6 %all-to-all-done.4 = f32[16,4,2,128]{3,2,1,0:T(2,128)S(1)} async-done(((f32[16,4,2,128]{3,2,1,0:T(2,128)}), f32[16,4,2,128]{3,2,1,0:T(2,128)S(1)}, u32[]{:S(2)}, u32[]{:S(2)}) %all-to-all-start.4) | async-done | bytes 65568 | tf_op jit(solution)/shard_map/all_to_all | solution.py:44
  197.6 9.5 %shard_map.104 = bf16[64,3072]{1,0:T(8,128)(2,1)S(1)} custom-call(bf16[64,3072]{1,0:T(8,128)(2,1)S(1)} %bitcast.61, f32[3,3072]{1,0:T(4,128)S(1)} %reshape.80.mod_ref, bf16[192,3072]{1,0:T(8,128)(2,1)S(1)} %get-tuple-element.12.refs_0_, bf16[192,3072]{1,0:T(8,128)(2,1)S(1)} %get-tuple-element.13.refs_1_, bf16[192,3072]{1,0:T(8,128)(2,1)S(1)} %copy-done.2, ...), custom_call_target="tpu_custom_call" | custom-call | flops 1207959552 | bytes 19660800 | tf_op jit(solution)/shard_map/pallas_call | solution.py:104
  207.9 4.2 %all-to-all-start.5 = ((bf16[8,8,3072]{2,1,0:T(8,128)(2,1)}), bf16[8,8,3072]{2,1,0:T(8,128)(2,1)}, u32[]{:S(2)}, u32[]{:S(2)}) async-start(bf16[8,8,3072]{2,1,0:T(8,128)(2,1)} %bitcast.62), calls=%async_computation.5 | async-start | bytes 786432 | tf_op jit(solution)/shard_map/all_to_all | solution.py:247
  213.5 8.8 %all-to-all-done.5.parts_ref = bf16[8,8,3072]{2,1,0:T(8,128)(2,1)} async-done(((bf16[8,8,3072]{2,1,0:T(8,128)(2,1)}), bf16[8,8,3072]{2,1,0:T(8,128)(2,1)}, u32[]{:S(2)}, u32[]{:S(2)}) %all-to-all-start.5) | async-done | bytes 393248 | tf_op jit(solution)/shard_map/all_to_all | solution.py:247
  222.3 1.7 shard_map.105
  224.0 10.6 %collective-permute-start.16 = (bf16[8,3200]{1,0:T(8,128)(2,1)}, bf16[8,3200]{1,0:T(8,128)(2,1)S(1)}, u32[]{:S(2)}, u32[]{:S(2)}) collective-permute-start(bf16[8,3200]{1,0:T(8,128)(2,1)} %shard_map.105), channel_id=1, source_target_pairs={{0,64},{2,66},{64,130},{66,128},{128,192},{130,194},{1,65},{3,67},... | collective-permute-start | bytes 153608 | tf_op jit(solution)/shard_map/ppermute | solution.py:34
  234.7 1.7 collective-permute-done.16
  237.9 13.8 %all_to_all.62 = bf16[8,8,3072]{2,1,0:T(8,128)(2,1)S(1)} all-to-all(bf16[8,8,3072]{2,1,0:T(8,128)(2,1)S(1)} %broadcast_in_dim.34), channel_id=1, replica_groups=mesh['zh'=2,'core'=2,'xh'=2,'xl'=2,'yh'=2,'yl'=2,'zc'=2,'zf'=2] {'xh','z..., dimensions={0} | all-to-all | bytes 786432 | tf_op jit(solution)/shard_map/all_to_all | solution.py:44
  251.7 1.3 copy-done.8
  254.2 9.5 %shard_map.106 = bf16[64,3072]{1,0:T(8,128)(2,1)S(1)} custom-call(bf16[64,3072]{1,0:T(8,128)(2,1)S(1)} %bitcast.65, f32[3,3072]{1,0:T(4,128)S(1)} %reshape.80.mod_ref, bf16[192,3072]{1,0:T(8,128)(2,1)S(1)} %get-tuple-element.12.refs_0_, bf16[192,3072]{1,0:T(8,128)(2,1)S(1)} %get-tuple-element.13.refs_1_, bf16[192,3072]{1,0:T(8,128)(2,1)S(1)} %copy-done.3, ...), custom_call_target="tpu_custom_call" | custom-call | flops 1207959552 | bytes 19660800 | tf_op jit(solution)/shard_map/pallas_call | solution.py:104
  264.5 4.1 %all-to-all-start.7 = ((bf16[8,8,3072]{2,1,0:T(8,128)(2,1)}), bf16[8,8,3072]{2,1,0:T(8,128)(2,1)}, u32[]{:S(2)}, u32[]{:S(2)}) async-start(bf16[8,8,3072]{2,1,0:T(8,128)(2,1)} %bitcast.63), calls=%async_computation.7 | async-start | bytes 786432 | tf_op jit(solution)/shard_map/all_to_all | solution.py:247
  268.6 1.3 collective-permute-start
  269.9 10.0 %all-to-all-done.7.parts_ref = bf16[8,8,3072]{2,1,0:T(8,128)(2,1)} async-done(((bf16[8,8,3072]{2,1,0:T(8,128)(2,1)}), bf16[8,8,3072]{2,1,0:T(8,128)(2,1)}, u32[]{:S(2)}, u32[]{:S(2)}) %all-to-all-start.7) | async-done | bytes 393248 | tf_op jit(solution)/shard_map/all_to_all | solution.py:247
  280.0 1.7 shard_map.107
  281.7 6.0 %collective-permute-start.17 = (bf16[8,3200]{1,0:T(8,128)(2,1)}, bf16[8,3200]{1,0:T(8,128)(2,1)S(1)}, u32[]{:S(2)}, u32[]{:S(2)}) collective-permute-start(bf16[8,3200]{1,0:T(8,128)(2,1)} %shard_map.107), channel_id=1, source_target_pairs={{0,64},{2,66},{64,130},{66,128},{128,192},{130,194},{1,65},{3,67},... | collective-permute-start | bytes 153608 | tf_op jit(solution)/shard_map/ppermute | solution.py:34
  289.5 13.9 %all_to_all.63 = bf16[8,8,3072]{2,1,0:T(8,128)(2,1)S(1)} all-to-all(bf16[8,8,3072]{2,1,0:T(8,128)(2,1)S(1)} %broadcast_in_dim.35), channel_id=1, replica_groups=mesh['zh'=2,'core'=2,'xh'=2,'xl'=2,'yh'=2,'yl'=2,'zc'=2,'zf'=2] {'xh','z..., dimensions={0} | all-to-all | bytes 786432 | tf_op jit(solution)/shard_map/all_to_all | solution.py:44
  303.4 1.3 copy-done.9
  305.9 9.5 %shard_map.108 = bf16[64,3072]{1,0:T(8,128)(2,1)S(1)} custom-call(bf16[64,3072]{1,0:T(8,128)(2,1)S(1)} %bitcast.66, f32[3,3072]{1,0:T(4,128)S(1)} %reshape.80.mod_ref, bf16[192,3072]{1,0:T(8,128)(2,1)S(1)} %get-tuple-element.12.refs_0_, bf16[192,3072]{1,0:T(8,128)(2,1)S(1)} %get-tuple-element.13.refs_1_, bf16[192,3072]{1,0:T(8,128)(2,1)S(1)} %copy-done.4, ...), custom_call_target="tpu_custom_call" | custom-call | flops 1207959552 | bytes 19660800 | tf_op jit(solution)/shard_map/pallas_call | solution.py:104
  316.2 4.1 %all-to-all-start.9 = ((bf16[8,8,3072]{2,1,0:T(8,128)(2,1)}), bf16[8,8,3072]{2,1,0:T(8,128)(2,1)}, u32[]{:S(2)}, u32[]{:S(2)}) async-start(bf16[8,8,3072]{2,1,0:T(8,128)(2,1)} %bitcast.64), calls=%async_computation.9 | async-start | bytes 786432 | tf_op jit(solution)/shard_map/all_to_all | solution.py:247
  321.0 10.8 %all-to-all-done.9.parts_ref = bf16[8,8,3072]{2,1,0:T(8,128)(2,1)} async-done(((bf16[8,8,3072]{2,1,0:T(8,128)(2,1)}), bf16[8,8,3072]{2,1,0:T(8,128)(2,1)}, u32[]{:S(2)}, u32[]{:S(2)}) %all-to-all-start.9) | async-done | bytes 393248 | tf_op jit(solution)/shard_map/all_to_all | solution.py:247
  331.8 1.7 shard_map.109
  333.6 6.2 %collective-permute-start.22 = (bf16[8,3200]{1,0:T(8,128)(2,1)}, bf16[8,3200]{1,0:T(8,128)(2,1)S(1)}, u32[]{:S(2)}, u32[]{:S(2)}) collective-permute-start(bf16[8,3200]{1,0:T(8,128)(2,1)} %shard_map.109), channel_id=1, source_target_pairs={{0,64},{2,66},{64,130},{66,128},{128,192},{130,194},{1,65},{3,67},... | collective-permute-start | bytes 153608 | tf_op jit(solution)/shard_map/ppermute | solution.py:34
  341.4 14.6 %all_to_all.64 = bf16[8,8,3072]{2,1,0:T(8,128)(2,1)S(1)} all-to-all(bf16[8,8,3072]{2,1,0:T(8,128)(2,1)S(1)} %broadcast_in_dim.36), channel_id=1, replica_groups=mesh['zh'=2,'core'=2,'xh'=2,'xl'=2,'yh'=2,'yl'=2,'zc'=2,'zf'=2] {'xh','z..., dimensions={0} | all-to-all | bytes 786432 | tf_op jit(solution)/shard_map/all_to_all | solution.py:44
  356.0 1.3 copy-done.10
  358.5 9.5 %shard_map.110 = bf16[64,3072]{1,0:T(8,128)(2,1)S(1)} custom-call(bf16[64,3072]{1,0:T(8,128)(2,1)S(1)} %bitcast.60, f32[3,3072]{1,0:T(4,128)S(1)} %reshape.80.mod_ref, bf16[192,3072]{1,0:T(8,128)(2,1)S(1)} %get-tuple-element.12.refs_0_, bf16[192,3072]{1,0:T(8,128)(2,1)S(1)} %get-tuple-element.13.refs_1_, bf16[192,3072]{1,0:T(8,128)(2,1)S(1)} %copy-done.5, ...), custom_call_target="tpu_custom_call" | custom-call | flops 1207959552 | bytes 19660800 | tf_op jit(solution)/shard_map/pallas_call | solution.py:104
  368.8 3.6 all-to-all-start.11
  373.9 1.3 collective-permute-start.19
  376.7 8.8 %all-to-all-done.11.parts_ref = bf16[8,8,3072]{2,1,0:T(8,128)(2,1)S(1)} async-done(((bf16[8,8,3072]{2,1,0:T(8,128)(2,1)}), bf16[8,8,3072]{2,1,0:T(8,128)(2,1)S(1)}, u32[]{:S(2)}, u32[]{:S(2)}) %all-to-all-start.11) | async-done | bytes 393248 | tf_op jit(solution)/shard_map/all_to_all | solution.py:247
  386.2 1.7 shard_map.111
  390.1 6.6 %collective-permute-start.25 = (bf16[8,3200]{1,0:T(8,128)(2,1)}, bf16[8,3200]{1,0:T(8,128)(2,1)S(1)}, u32[]{:S(2)}, u32[]{:S(2)}) collective-permute-start(bf16[8,3200]{1,0:T(8,128)(2,1)} %shard_map.111), channel_id=1, source_target_pairs={{0,64},{2,66},{64,128},{66,130},{128,194},{130,192},{1,65},{3,67},... | collective-permute-start | bytes 153608 | tf_op jit(solution)/shard_map/ppermute | solution.py:34
  (147 shorter events, 39.9 us)
Async XLA Ops:
  0.6 40.8 %copy-start = (bf16[1,144,3584]{2,1,0:T(8,128)(2,1)S(1)}, bf16[1,144,3584]{2,1,0:T(8,128)(2,1)}, u32[]{:S(2)}) copy-start(bf16[1,144,3584]{2,1,0:T(8,128)(2,1)} %param.15) | copy-start | bytes 3096580
  3.1 15.0 %all-to-all-start = ((f32[16,28,128]{2,1,0:T(8,128)}), f32[16,28,128]{2,1,0:T(8,128)S(1)}, u32[]{:S(2)}, u32[]{:S(2)}) async-start(f32[16,28,128]{2,1,0:T(8,128)} %broadcast_in_dim.27), calls=%async_computation | async-start | bytes 524288 | tf_op jit(solution)/shard_map/all_to_all | solution.py:44
  10.7 18.7 %copy-start.21 = (bf16[1,192,3072]{2,1,0:T(8,128)(2,1)S(1)}, bf16[1,192,3072]{2,1,0:T(8,128)(2,1)}, u32[]{:S(2)}) copy-start(bf16[1,192,3072]{2,1,0:T(8,128)(2,1)} %param.16) | copy-start | bytes 3538948
  18.9 20.2 %all-to-all-start.1 = ((f32[16,28,128]{2,1,0:T(8,128)}), f32[16,28,128]{2,1,0:T(8,128)}, u32[]{:S(2)}, u32[]{:S(2)}) async-start(f32[16,28,128]{2,1,0:T(8,128)} %broadcast_in_dim.28), calls=%async_computation.1 | async-start | bytes 524288 | tf_op jit(solution)/shard_map/all_to_all | solution.py:44
  32.3 18.2 %copy-start.29 = (bf16[1,8,3072]{2,1,0:T(8,128)(2,1)S(1)}, bf16[1,8,3072]{2,1,0:T(8,128)(2,1)}, u32[]{:S(2)}) copy-start(bf16[1,8,3072]{2,1,0:T(8,128)(2,1)} %param.9) | copy-start | bytes 147460
  32.3 53.7 %collective-permute-start.5 = (bf16[192,3072]{1,0:T(8,128)(2,1)S(1)}, bf16[192,3072]{1,0:T(8,128)(2,1)}, u32[]{:S(2)}, u32[]{:S(2)}) collective-permute-start(bf16[192,3072]{1,0:T(8,128)(2,1)S(1)} %get-tuple-element.13.refs_1_), channel_id=1, source_target_pairs={{12,0},{0,4},{4,8},{8,12},{13,1},{1,5},{5,9},{9,13},{14,2},{2,6},{... | collective-permute-start | bytes 3538952 | tf_op jit(solution)/shard_map/ppermute | solution.py:27
  32.6 54.1 %collective-permute-start.6 = (bf16[192,3072]{1,0:T(8,128)(2,1)S(1)}, bf16[192,3072]{1,0:T(8,128)(2,1)}, u32[]{:S(2)}, u32[]{:S(2)}) collective-permute-start(bf16[192,3072]{1,0:T(8,128)(2,1)S(1)} %get-tuple-element.13.refs_1_), channel_id=1, source_target_pairs={{4,0},{8,4},{12,8},{0,12},{5,1},{9,5},{13,9},{1,13},{6,2},{10,6},{... | collective-permute-start | bytes 3538952 | tf_op jit(solution)/shard_map/ppermute | solution.py:27
  35.0 50.2 %collective-permute-start.4 = (bf16[192,3072]{1,0:T(8,128)(2,1)S(1)}, bf16[192,3072]{1,0:T(8,128)(2,1)}, u32[]{:S(2)}, u32[]{:S(2)}) collective-permute-start(bf16[192,3072]{1,0:T(8,128)(2,1)S(1)} %get-tuple-element.12.refs_0_), channel_id=1, source_target_pairs={{4,0},{8,4},{12,8},{0,12},{5,1},{9,5},{13,9},{1,13},{6,2},{10,6},{... | collective-permute-start | bytes 3538952 | tf_op jit(solution)/shard_map/ppermute | solution.py:27
  35.1 53.6 %collective-permute-start.7 = (bf16[192,3072]{1,0:T(8,128)(2,1)S(1)}, bf16[192,3072]{1,0:T(8,128)(2,1)}, u32[]{:S(2)}, u32[]{:S(2)}) collective-permute-start(bf16[192,3072]{1,0:T(8,128)(2,1)S(1)} %get-tuple-element.12.refs_0_), channel_id=1, source_target_pairs={{12,0},{0,4},{4,8},{8,12},{13,1},{1,5},{5,9},{9,13},{14,2},{2,6},{... | collective-permute-start | bytes 3538952 | tf_op jit(solution)/shard_map/ppermute | solution.py:27
  58.6 78.2 %copy-start.22 = (bf16[4,8,3072]{2,1,0:T(8,128)(2,1)}, bf16[4,8,3072]{2,1,0:T(8,128)(2,1)S(1)}, u32[]{:S(2)}) copy-start(bf16[4,8,3072]{2,1,0:T(8,128)(2,1)S(1)} %all_to_all.61) | copy-start | bytes 589828
  58.6 33.6 %collective-permute-start.1 = (bf16[4,8,3072]{2,1,0:T(8,128)(2,1)S(1)}, bf16[4,8,3072]{2,1,0:T(8,128)(2,1)S(1)}, u32[]{:S(2)}, u32[]{:S(2)}) collective-permute-start(bf16[4,8,3072]{2,1,0:T(8,128)(2,1)S(1)} %all_to_all.61), channel_id=1, source_target_pairs={{0,32},{32,0},{1,33},{33,1},{2,34},{34,2},{3,35},{35,3},{4,36},{36... | collective-permute-start | bytes 589832 | tf_op jit(solution)/shard_map/ppermute | solution.py:199
  85.2 26.3 %collective-permute-start.2 = (bf16[192,3072]{1,0:T(8,128)(2,1)S(1)}, bf16[192,3072]{1,0:T(8,128)(2,1)S(1)}, u32[]{:S(2)}, u32[]{:S(2)}) collective-permute-start(bf16[192,3072]{1,0:T(8,128)(2,1)S(1)} %get-tuple-element.12.refs_0_), channel_id=1, source_target_pairs={{16,0},{32,16},{48,32},{0,48},{17,1},{33,17},{49,33},{1,49},{18,2}... | collective-permute-start | bytes 3538952 | tf_op jit(solution)/shard_map/ppermute | solution.py:27
  86.0 27.2 %collective-permute-start.3 = (bf16[192,3072]{1,0:T(8,128)(2,1)S(1)}, bf16[192,3072]{1,0:T(8,128)(2,1)S(1)}, u32[]{:S(2)}, u32[]{:S(2)}) collective-permute-start(bf16[192,3072]{1,0:T(8,128)(2,1)S(1)} %get-tuple-element.13.refs_1_), channel_id=1, source_target_pairs={{48,0},{0,16},{16,32},{32,48},{49,1},{1,17},{17,33},{33,49},{50,2}... | collective-permute-start | bytes 3538952 | tf_op jit(solution)/shard_map/ppermute | solution.py:27
  86.7 50.1 %collective-permute-start.8 = (bf16[192,3072]{1,0:T(8,128)(2,1)}, bf16[192,3072]{1,0:T(8,128)(2,1)S(1)}, u32[]{:S(2)}, u32[]{:S(2)}) collective-permute-start(bf16[192,3072]{1,0:T(8,128)(2,1)} %collective-permute-done.4.refs_4_), channel_id=1, source_target_pairs={{16,0},{32,16},{48,32},{0,48},{17,1},{33,17},{49,33},{1,49},{18,2}... | collective-permute-start | bytes 3538952 | tf_op jit(solution)/shard_map/ppermute | solution.py:27
  88.7 49.2 %collective-permute-start.10 = (bf16[192,3072]{1,0:T(8,128)(2,1)}, bf16[192,3072]{1,0:T(8,128)(2,1)}, u32[]{:S(2)}, u32[]{:S(2)}) collective-permute-start(bf16[192,3072]{1,0:T(8,128)(2,1)} %collective-permute-done.4.refs_4_), channel_id=1, source_target_pairs={{4,0},{8,4},{12,8},{0,12},{5,1},{9,5},{13,9},{1,13},{6,2},{10,6},{... | collective-permute-start | bytes 3538952 | tf_op jit(solution)/shard_map/ppermute | solution.py:27
  92.2 45.6 %copy-start.28 = (bf16[4,8,3072]{2,1,0:T(8,128)(2,1)}, bf16[4,8,3072]{2,1,0:T(8,128)(2,1)S(1)}, u32[]{:S(2)}) copy-start(bf16[4,8,3072]{2,1,0:T(8,128)(2,1)S(1)} %collective-permute-done.1) | copy-start | bytes 589828
  92.2 48.3 %collective-permute-start.11 = (bf16[192,3072]{1,0:T(8,128)(2,1)}, bf16[192,3072]{1,0:T(8,128)(2,1)}, u32[]{:S(2)}, u32[]{:S(2)}) collective-permute-start(bf16[192,3072]{1,0:T(8,128)(2,1)} %collective-permute-done.5.refs_5_), channel_id=1, source_target_pairs={{12,0},{0,4},{4,8},{8,12},{13,1},{1,5},{5,9},{9,13},{14,2},{2,6},{... | collective-permute-start | bytes 3538952 | tf_op jit(solution)/shard_map/ppermute | solution.py:27
  112.5 82.3 %collective-permute-start.9 = (bf16[192,3072]{1,0:T(8,128)(2,1)}, bf16[192,3072]{1,0:T(8,128)(2,1)}, u32[]{:S(2)}, u32[]{:S(2)}) collective-permute-start(bf16[192,3072]{1,0:T(8,128)(2,1)} %collective-permute-done.5.refs_5_), channel_id=1, source_target_pairs={{48,0},{0,16},{16,32},{32,48},{49,1},{1,17},{17,33},{33,49},{50,2}... | collective-permute-start | bytes 3538952 | tf_op jit(solution)/shard_map/ppermute | solution.py:27
  114.3 80.6 %collective-permute-start.12 = (bf16[192,3072]{1,0:T(8,128)(2,1)}, bf16[192,3072]{1,0:T(8,128)(2,1)}, u32[]{:S(2)}, u32[]{:S(2)}) collective-permute-start(bf16[192,3072]{1,0:T(8,128)(2,1)} %collective-permute-done.7.refs_7_), channel_id=1, source_target_pairs={{16,0},{32,16},{48,32},{0,48},{17,1},{33,17},{49,33},{1,49},{18,2}... | collective-permute-start | bytes 3538952 | tf_op jit(solution)/shard_map/ppermute | solution.py:27
  137.8 57.0 %collective-permute-start.13 = (bf16[192,3072]{1,0:T(8,128)(2,1)}, bf16[192,3072]{1,0:T(8,128)(2,1)}, u32[]{:S(2)}, u32[]{:S(2)}) collective-permute-start(bf16[192,3072]{1,0:T(8,128)(2,1)} %collective-permute-done.6.refs_6_), channel_id=1, source_target_pairs={{48,0},{0,16},{16,32},{32,48},{49,1},{1,17},{17,33},{33,49},{50,2}... | collective-permute-start | bytes 3538952 | tf_op jit(solution)/shard_map/ppermute | solution.py:27
  137.8 57.0 %collective-permute-start.14 = (bf16[192,3072]{1,0:T(8,128)(2,1)}, bf16[192,3072]{1,0:T(8,128)(2,1)}, u32[]{:S(2)}, u32[]{:S(2)}) collective-permute-start(bf16[192,3072]{1,0:T(8,128)(2,1)} %collective-permute-done.10.refs_10_), channel_id=1, source_target_pairs={{16,0},{32,16},{48,32},{0,48},{17,1},{33,17},{49,33},{1,49},{18,2}... | collective-permute-start | bytes 3538952 | tf_op jit(solution)/shard_map/ppermute | solution.py:27
  140.5 54.4 %collective-permute-start.15 = (bf16[192,3072]{1,0:T(8,128)(2,1)}, bf16[192,3072]{1,0:T(8,128)(2,1)}, u32[]{:S(2)}, u32[]{:S(2)}) collective-permute-start(bf16[192,3072]{1,0:T(8,128)(2,1)} %collective-permute-done.11.refs_11_), channel_id=1, source_target_pairs={{48,0},{0,16},{16,32},{32,48},{49,1},{1,17},{17,33},{33,49},{50,2}... | collective-permute-start | bytes 3538952 | tf_op jit(solution)/shard_map/ppermute | solution.py:27
  141.2 50.9 %all-to-all-start.4 = ((f32[16,4,2,128]{3,2,1,0:T(2,128)}), f32[16,4,2,128]{3,2,1,0:T(2,128)S(1)}, u32[]{:S(2)}, u32[]{:S(2)}) async-start(f32[16,4,2,128]{3,2,1,0:T(2,128)} %broadcast_in_dim.32), calls=%async_computation.4 | async-start | bytes 131072 | tf_op jit(solution)/shard_map/all_to_all | solution.py:44
  197.6 14.5 %copy-start.35 = (s32[1,8]{1,0:T(1,128)S(1)}, s32[1,8]{1,0:T(1,128)}, u32[]{:S(2)}) copy-start(s32[1,8]{1,0:T(1,128)} %param.10) | copy-start | bytes 100
  207.9 26.7 %copy-start.36 = (s32[1,8]{1,0:T(1,128)S(1)}, s32[1,8]{1,0:T(1,128)}, u32[]{:S(2)}) copy-start(s32[1,8]{1,0:T(1,128)} %param.12) | copy-start | bytes 100
  207.9 14.4 %all-to-all-start.5 = ((bf16[8,8,3072]{2,1,0:T(8,128)(2,1)}), bf16[8,8,3072]{2,1,0:T(8,128)(2,1)}, u32[]{:S(2)}, u32[]{:S(2)}) async-start(bf16[8,8,3072]{2,1,0:T(8,128)(2,1)} %bitcast.62), calls=%async_computation.5 | async-start | bytes 786432 | tf_op jit(solution)/shard_map/all_to_all | solution.py:247
  224.0 12.4 %collective-permute-start.16 = (bf16[8,3200]{1,0:T(8,128)(2,1)}, bf16[8,3200]{1,0:T(8,128)(2,1)S(1)}, u32[]{:S(2)}, u32[]{:S(2)}) collective-permute-start(bf16[8,3200]{1,0:T(8,128)(2,1)} %shard_map.105), channel_id=1, source_target_pairs={{0,64},{2,66},{64,130},{66,128},{128,192},{130,194},{1,65},{3,67},... | collective-permute-start | bytes 153608 | tf_op jit(solution)/shard_map/ppermute | solution.py:34
  234.7 17.0 %copy-start.3 = (bf16[192,3072]{1,0:T(8,128)(2,1)S(1)}, bf16[192,3072]{1,0:T(8,128)(2,1)}, u32[]{:S(2)}) copy-start(bf16[192,3072]{1,0:T(8,128)(2,1)} %copy-done.1) | copy-start | bytes 3538948
  237.9 25.9 %copy-start.24 = (bf16[8,3200]{1,0:T(8,128)(2,1)}, bf16[8,3200]{1,0:T(8,128)(2,1)S(1)}, u32[]{:S(2)}) copy-start(bf16[8,3200]{1,0:T(8,128)(2,1)S(1)} %get-tuple-element.26.waiting_ref) | copy-start | bytes 153604
  237.9 82.4 %copy-start.30 = (bf16[8,3200]{1,0:T(8,128)(2,1)}, bf16[8,3200]{1,0:T(8,128)(2,1)S(1)}, u32[]{:S(2)}) copy-start(bf16[8,3200]{1,0:T(8,128)(2,1)S(1)} %get-tuple-element.27) | copy-start | bytes 153604
  264.5 15.4 %all-to-all-start.7 = ((bf16[8,8,3072]{2,1,0:T(8,128)(2,1)}), bf16[8,8,3072]{2,1,0:T(8,128)(2,1)}, u32[]{:S(2)}, u32[]{:S(2)}) async-start(bf16[8,8,3072]{2,1,0:T(8,128)(2,1)} %bitcast.63), calls=%async_computation.7 | async-start | bytes 786432 | tf_op jit(solution)/shard_map/all_to_all | solution.py:247
  268.6 19.0 %collective-permute-start = (bf16[8,3200]{1,0:T(8,128)(2,1)S(1)}, bf16[8,3200]{1,0:T(8,128)(2,1)S(1)}, u32[]{:S(2)}, u32[]{:S(2)}) collective-permute-start(bf16[8,3200]{1,0:T(8,128)(2,1)S(1)} %get-tuple-element.27), channel_id=1, source_target_pairs={{64,0},{66,2},{65,1},{67,3},{68,4},{70,6},{69,5},{71,7},{72,8},{74... | collective-permute-start | bytes 153608 | tf_op jit(solution)/shard_map/ppermute | solution.py:34
  281.7 21.7 %copy-start.4 = (bf16[192,3072]{1,0:T(8,128)(2,1)S(1)}, bf16[192,3072]{1,0:T(8,128)(2,1)}, u32[]{:S(2)}) copy-start(bf16[192,3072]{1,0:T(8,128)(2,1)} %copy-done.1) | copy-start | bytes 3538948
  281.7 7.8 %collective-permute-start.17 = (bf16[8,3200]{1,0:T(8,128)(2,1)}, bf16[8,3200]{1,0:T(8,128)(2,1)S(1)}, u32[]{:S(2)}, u32[]{:S(2)}) collective-permute-start(bf16[8,3200]{1,0:T(8,128)(2,1)} %shard_map.107), channel_id=1, source_target_pairs={{0,64},{2,66},{64,130},{66,128},{128,192},{130,194},{1,65},{3,67},... | collective-permute-start | bytes 153608 | tf_op jit(solution)/shard_map/ppermute | solution.py:34
  289.5 26.0 %copy-start.25 = (bf16[8,3200]{1,0:T(8,128)(2,1)}, bf16[8,3200]{1,0:T(8,128)(2,1)S(1)}, u32[]{:S(2)}) copy-start(bf16[8,3200]{1,0:T(8,128)(2,1)S(1)} %broadcast_select_fusion.1.waiting_ref) | copy-start | bytes 153604
  316.2 15.6 %all-to-all-start.9 = ((bf16[8,8,3072]{2,1,0:T(8,128)(2,1)}), bf16[8,8,3072]{2,1,0:T(8,128)(2,1)}, u32[]{:S(2)}, u32[]{:S(2)}) async-start(bf16[8,8,3072]{2,1,0:T(8,128)(2,1)} %bitcast.64), calls=%async_computation.9 | async-start | bytes 786432 | tf_op jit(solution)/shard_map/all_to_all | solution.py:247
  320.3 19.5 %collective-permute-start.21 = (bf16[8,3200]{1,0:T(8,128)(2,1)S(1)}, bf16[8,3200]{1,0:T(8,128)(2,1)S(1)}, u32[]{:S(2)}, u32[]{:S(2)}) collective-permute-start(bf16[8,3200]{1,0:T(8,128)(2,1)S(1)} %get-tuple-element.27), channel_id=1, source_target_pairs={{128,0},{130,2},{129,1},{131,3},{132,4},{134,6},{133,5},{135,7},{1... | collective-permute-start | bytes 153608 | tf_op jit(solution)/shard_map/ppermute | solution.py:34
  333.6 22.4 %copy-start.5 = (bf16[192,3072]{1,0:T(8,128)(2,1)S(1)}, bf16[192,3072]{1,0:T(8,128)(2,1)}, u32[]{:S(2)}) copy-start(bf16[192,3072]{1,0:T(8,128)(2,1)} %copy-done.1) | copy-start | bytes 3538948
  333.6 7.7 %collective-permute-start.22 = (bf16[8,3200]{1,0:T(8,128)(2,1)}, bf16[8,3200]{1,0:T(8,128)(2,1)S(1)}, u32[]{:S(2)}, u32[]{:S(2)}) collective-permute-start(bf16[8,3200]{1,0:T(8,128)(2,1)} %shard_map.109), channel_id=1, source_target_pairs={{0,64},{2,66},{64,130},{66,128},{128,192},{130,194},{1,65},{3,67},... | collective-permute-start | bytes 153608 | tf_op jit(solution)/shard_map/ppermute | solution.py:34
  341.3 26.8 %copy-start.23 = (bf16[8,3200]{1,0:T(8,128)(2,1)}, bf16[8,3200]{1,0:T(8,128)(2,1)S(1)}, u32[]{:S(2)}) copy-start(bf16[8,3200]{1,0:T(8,128)(2,1)S(1)} %broadcast_select_fusion.waiting_ref) | copy-start | bytes 153604
  368.8 20.6 %copy-start.31 = (bf16[8,3200]{1,0:T(8,128)(2,1)S(1)}, bf16[8,3200]{1,0:T(8,128)(2,1)}, u32[]{:S(2)}) copy-start(bf16[8,3200]{1,0:T(8,128)(2,1)} %copy-done.30) | copy-start | bytes 153604
  368.8 16.6 %all-to-all-start.11 = ((bf16[8,8,3072]{2,1,0:T(8,128)(2,1)}), bf16[8,8,3072]{2,1,0:T(8,128)(2,1)S(1)}, u32[]{:S(2)}, u32[]{:S(2)}) async-start(bf16[8,8,3072]{2,1,0:T(8,128)(2,1)} %bitcast.59), calls=%async_computation.11 | async-start | bytes 786432 | tf_op jit(solution)/shard_map/all_to_all | solution.py:247
  372.5 17.7 %collective-permute-start.20 = (bf16[8,3072]{1,0:T(8,128)(2,1)S(1)}, bf16[8,3072]{1,0:T(8,128)(2,1)S(1)}, u32[]{:S(2)}, u32[]{:S(2)}) collective-permute-start(bf16[8,3072]{1,0:T(8,128)(2,1)S(1)} %slice.81), channel_id=1, source_target_pairs={{192,0},{194,2},{193,1},{195,3},{196,4},{198,6},{197,5},{199,7},{2... | collective-permute-start | bytes 147464 | tf_op jit(solution)/shard_map/ppermute | solution.py:34
  373.9 22.8 %collective-permute-start.19 = (bf16[8,3072]{1,0:T(8,128)(2,1)S(1)}, bf16[8,3072]{1,0:T(8,128)(2,1)S(1)}, u32[]{:S(2)}, u32[]{:S(2)}) collective-permute-start(bf16[8,3072]{1,0:T(8,128)(2,1)S(1)} %slice.80), channel_id=1, source_target_pairs={{192,64},{194,66},{193,65},{195,67},{196,68},{198,70},{197,69},{19... | collective-permute-start | bytes 147464 | tf_op jit(solution)/shard_map/ppermute | solution.py:34
  376.0 20.7 %collective-permute-start.18 = (bf16[8,3072]{1,0:T(8,128)(2,1)S(1)}, bf16[8,3072]{1,0:T(8,128)(2,1)S(1)}, u32[]{:S(2)}, u32[]{:S(2)}) collective-permute-start(bf16[8,3072]{1,0:T(8,128)(2,1)S(1)} %slice.79), channel_id=1, source_target_pairs={{192,130},{194,128},{193,131},{195,129},{196,134},{198,132},{197,1... | collective-permute-start | bytes 147464 | tf_op jit(solution)/shard_map/ppermute | solution.py:34
  388.8 8.0 %collective-permute-start.23 = (bf16[8,3072]{1,0:T(8,128)(2,1)S(1)}, bf16[8,3072]{1,0:T(8,128)(2,1)S(1)}, u32[]{:S(2)}, u32[]{:S(2)}) collective-permute-start(bf16[8,3072]{1,0:T(8,128)(2,1)S(1)} %slice.83), channel_id=1, source_target_pairs={{192,194},{194,192},{193,195},{195,193},{196,198},{198,196},{197,1... | collective-permute-start | bytes 147464 | tf_op jit(solution)/shard_map/ppermute | solution.py:34
  389.5 7.9 %collective-permute-start.24 = (bf16[8,3200]{1,0:T(8,128)(2,1)S(1)}, bf16[8,3200]{1,0:T(8,128)(2,1)S(1)}, u32[]{:S(2)}, u32[]{:S(2)}) collective-permute-start(bf16[8,3200]{1,0:T(8,128)(2,1)S(1)} %copy-done.31), channel_id=1, source_target_pairs={{192,0},{194,2},{193,1},{195,3},{196,4},{198,6},{197,5},{199,7},{2... | collective-permute-start | bytes 153608 | tf_op jit(solution)/shard_map/ppermute | solution.py:34
  390.1 8.1 %collective-permute-start.25 = (bf16[8,3200]{1,0:T(8,128)(2,1)}, bf16[8,3200]{1,0:T(8,128)(2,1)S(1)}, u32[]{:S(2)}, u32[]{:S(2)}) collective-permute-start(bf16[8,3200]{1,0:T(8,128)(2,1)} %shard_map.111), channel_id=1, source_target_pairs={{0,64},{2,66},{64,128},{66,130},{128,194},{130,192},{1,65},{3,67},... | collective-permute-start | bytes 153608 | tf_op jit(solution)/shard_map/ppermute | solution.py:34
  (22 other events, 34.9 us)
